TPU v7x, 32 devices: a whole 2x2x4 slice. The times are simulated.
32 devices in a mesh: img: 8 (over y, x, core), rows: 4 (over z).
Axes of the slice: x: 2, y: 2, z: 4, core: 2. Of those that a mesh axis runs over, the one named last changes fastest.
Arguments:
- image_in: bfloat16 [640, 16, 16, 1024], P('img', 'rows'), may hold values from -8 to 8, as said below
- extent: int32 [640], P('img'), may hold values from 6 to 14, as said below
- weight_in1: bfloat16 [1024, 512], replicated, may hold values from -0.1875 to 0.1875
- weight_mid1: bfloat16 [512, 3, 3, 512], replicated, may hold values from -0.09375 to 0.09375
- weight_out1: bfloat16 [512, 2048], replicated, may hold values from -0.25 to 0.25
- weight_skip: bfloat16 [1024, 2048], replicated, may hold values from -0.1875 to 0.1875
- weight_in2: bfloat16 [2048, 512], replicated, may hold values from -0.125 to 0.125
- weight_mid2: bfloat16 [512, 3, 3, 512], replicated, may hold values from -0.09375 to 0.09375
- weight_out2: bfloat16 [512, 2048], replicated, may hold values from -0.25 to 0.25
- gain_in1: float32 [512], replicated, may hold values from 0.5 to 1.5
- shift_in1: float32 [512], replicated, may hold values from 0.2 to 1.2
- gain_mid1: float32 [512], replicated, may hold values from 0.5 to 1.5
- shift_mid1: float32 [512], replicated, may hold values from 0.2 to 1.2
- gain_out1: float32 [2048], replicated, may hold values from 0.5 to 1.5
- shift_out1: float32 [2048], replicated, may hold values from 0.2 to 1.2
- gain_skip: float32 [2048], replicated, may hold values from 0.5 to 1.5
- shift_skip: float32 [2048], replicated, may hold values from 0.2 to 1.2
- gain_in2: float32 [512], replicated, may hold values from 0.5 to 1.5
- shift_in2: float32 [512], replicated, may hold values from 0.2 to 1.2
- gain_mid2: float32 [512], replicated, may hold values from 0.5 to 1.5
- shift_mid2: float32 [512], replicated, may hold values from 0.2 to 1.2
- gain_out2: float32 [2048], replicated, may hold values from 0.5 to 1.5
- shift_out2: float32 [2048], replicated, may hold values from 0.2 to 1.2
- cotangent: bfloat16 [640, 8, 8, 2048], P('img', 'rows'), may hold values from -6 to 6
Outputs:
- block_out: bfloat16 [640, 8, 8, 2048], P('img', 'rows')
- grad_image: bfloat16 [640, 16, 16, 1024], P('img', 'rows')
- grad_weight_in1: float32 [1024, 512], P('img')
- grad_weight_mid1: float32 [512, 3, 3, 512], P('img')
- grad_weight_out1: float32 [512, 2048], P('img')
- grad_weight_skip: float32 [1024, 2048], P('img')
- grad_weight_in2: float32 [2048, 512], P('img')
- grad_weight_mid2: float32 [512, 3, 3, 512], P('img')
- grad_weight_out2: float32 [512, 2048], P('img')
- grad_gain_in1: float32 [512], replicated
- grad_shift_in1: float32 [512], replicated
- grad_gain_mid1: float32 [512], replicated
- grad_shift_mid1: float32 [512], replicated
- grad_gain_out1: float32 [2048], replicated
- grad_shift_out1: float32 [2048], replicated
- grad_gain_skip: float32 [2048], replicated
- grad_shift_skip: float32 [2048], replicated
- grad_gain_in2: float32 [512], replicated
- grad_shift_in2: float32 [512], replicated
- grad_gain_mid2: float32 [512], replicated
- grad_shift_mid2: float32 [512], replicated
- grad_gain_out2: float32 [2048], replicated
- grad_shift_out2: float32 [2048], replicated
Inputs may be any that keep to these rules, and one draw needn't show every extreme that they name: `extent`: each image's valid height and width within its padded map: 14 for a global view or 6 for a small crop, and both kinds occur in every draw; pixels at or past it are padding. `image_in`: activations of the previous section; padding pixels hold values that the mask removes.
All inputs are finite; a program needn't handle non-finite values.
Results may differ from a plain program's by a relative error of at most 0.02.
Values may be sent and summed in bfloat16 or wider, within the bound.
A program may use at most 384 MiB of HBM per device.

v0:
```python
import functools

import jax
import jax.numpy as jnp
import numpy as np
from jax import lax
from jax.experimental import pallas as pl
from jax.experimental.pallas import tpu as pltpu
from jax.sharding import PartitionSpec as P

EPSILON = 1e-05
F32 = jnp.float32
BF16 = jnp.bfloat16
LANES = 512
ROWS = 32
IMAGES = 16
VMEM_BYTES = 56 * 1024 * 1024
MESH = pl.DeviceIdType.MESH


def dot(a, b):
    return jnp.dot(a, b, preferred_element_type=F32)


def dot_t(a, b):
    return lax.dot_general(a, b, (((1,), (1,)), ((), ())), preferred_element_type=F32)


def load(ref, rows, lanes):
    value = ref[rows, lanes].astype(F32)
    return value.reshape(value.shape[0] // 8, 8, value.shape[1])


def store(ref, rows, lanes, value):
    ref[rows, lanes] = value.reshape(value.shape[0] * 8, value.shape[2]).astype(ref.dtype)


def load_mask(ref, rows):
    mask = load(ref, rows, slice(None))
    return jnp.concatenate([mask] * (LANES // 128), axis=-1)


def sweep(total, step, init, rows=ROWS):
    def body(i, carry):
        return step(pl.ds(pl.multiple_of(i * rows, rows), rows), i, carry)

    return lax.fori_loop(0, total // rows, body, init)


def lane_blocks(width):
    return [slice(k * LANES, (k + 1) * LANES) for k in range(width // LANES)]


def tall(row):
    return jnp.broadcast_to(row, (8, row.shape[-1]))


def column_sum(value):
    return jnp.sum(value, axis=0)


def total_of(part):
    return jnp.sum(part, axis=0, keepdims=True)


def zeros8():
    return jnp.zeros((8, LANES), F32)


def tally(first, parts, centre_ref, stats_ref):
    width = parts[0][0].shape[-1]

    @pl.when(first)
    def _():
        stats_ref[...] = jnp.zeros_like(stats_ref)

    for lanes in lane_blocks(width):
        sums = (zeros8(), zeros8())
        for acc, mask_ref, dev in parts:

            def add(rows, i, carry, acc=acc, mask_ref=mask_ref):
                mask = load_mask(mask_ref, rows)
                return (
                    carry[0] + column_sum(load(acc, rows, lanes) * mask),
                    carry[1] + column_sum(mask),
                )

            sums = sweep(acc.shape[0], add, sums)
        total, count = total_of(sums[0]), total_of(sums[1])
        centre = total / jnp.maximum(count, 1.0)
        centre_ref[:, lanes] = centre
        centre8 = tall(centre)
        squares = zeros8()
        for acc, mask_ref, dev in parts:

            def square(rows, i, carry, acc=acc, mask_ref=mask_ref, dev=dev):
                away = load(acc, rows, lanes) - centre8
                store(dev, rows, lanes, away)
                return carry + column_sum(load_mask(mask_ref, rows) * away * away)

            squares = sweep(acc.shape[0], square, squares)
        squares = total_of(squares)
        count_old, mean_old, squares_old = (
            stats_ref[0:1, lanes],
            stats_ref[1:2, lanes],
            stats_ref[2:3, lanes],
        )
        both = count_old + count
        share = count / jnp.maximum(both, 1.0)
        delta = centre - mean_old
        stats_ref[0:1, lanes] = both
        stats_ref[1:2, lanes] = mean_old + delta * share
        stats_ref[2:3, lanes] = squares_old + squares + delta * delta * count_old * share


def affine(stats_ref, gain_ref, shift_ref, centre_ref, lanes):
    scale = lax.rsqrt(stats_ref[2:3, lanes] + EPSILON)
    slope = gain_ref[:, lanes] * scale
    base = shift_ref[:, lanes] + (centre_ref[:, lanes] - stats_ref[1:2, lanes]) * slope
    return tall(0.5 * slope), tall(0.5 * base)


def silu_half(half):
    return half + half * jnp.tanh(half)


def gate_half(half):
    tanh = jnp.tanh(half)
    return (0.5 + 0.5 * tanh) * (1.0 + half * (1.0 - tanh))


def silu_and_gate(half):
    tanh = jnp.tanh(half)
    return half + half * tanh, (0.5 + 0.5 * tanh) * (1.0 + half * (1.0 - tanh))


def back_coefs(stats_ref, gain_ref, centre_ref, sums, lanes):
    shift_sum, gain_sum = sums
    pixels = stats_ref[0:1, lanes]
    scale = lax.rsqrt(stats_ref[2:3, lanes] + EPSILON)
    slope = gain_ref[:, lanes] * scale
    per_pixel = slope / pixels
    away = (centre_ref[:, lanes] - stats_ref[1:2, lanes]) * scale
    return (
        tall(slope),
        tall(-per_pixel * scale * gain_sum),
        tall(-per_pixel * (shift_sum + away * gain_sum)),
    )


def unit_sum(stats_ref, centre_ref, lanes, gn_sum, gd_sum):
    scale = lax.rsqrt(stats_ref[2:3, lanes] + EPSILON)
    return scale * (gd_sum + (centre_ref[:, lanes] - stats_ref[1:2, lanes]) * gn_sum)


def accumulate(first, ref, row, lanes, value):
    old = jnp.where(first, jnp.zeros_like(value), ref[row : row + 1, lanes])
    ref[row : row + 1, lanes] = old + value


def shifted(value, by):
    if by == 0:
        return value
    rolled = pltpu.roll(value, (-by) % 8, axis=1)
    column = lax.broadcasted_iota(jnp.int32, value.shape, 1)
    return jnp.where(column == (0 if by < 0 else 7), 0.0, rolled)


def from_above(value, edge, rows_low):
    if rows_low == 1:
        return edge
    images = value.shape[0] // rows_low
    image = value.reshape((images, rows_low) + value.shape[1:])
    return jnp.concatenate([edge[:, None], image[:, :-1]], axis=1).reshape(value.shape)


def from_below(value, edge, rows_low):
    if rows_low == 1:
        return edge
    images = value.shape[0] // rows_low
    image = value.reshape((images, rows_low) + value.shape[1:])
    return jnp.concatenate([image[:, 1:], edge[:, None]], axis=1).reshape(value.shape)


def edge_rows(i, rows_low):
    return pl.ds(pl.multiple_of(i * (ROWS // rows_low), ROWS // rows_low), ROWS // rows_low)


def first_step():
    return pl.program_id(0) == 0


def split_kernel(image_ref, perm_ref, mask_ref, weight_ref, planes_ref, dev_ref, centre_ref, stats_ref, acc):
    planes, low, _ = planes_ref.shape
    group = perm_ref.shape[0]
    part = group // planes
    for g in range(image_ref.shape[0] // group):
        mask = jnp.concatenate(
            [mask_ref[p, g * part : (g + 1) * part, :] for p in range(planes)], axis=0
        )
        mask = jnp.concatenate([mask] * (group // 128), axis=1)
        perm = (perm_ref[...].astype(F32) * mask).astype(BF16)
        moved = dot(perm, image_ref[g * group : (g + 1) * group, :]).astype(BF16)
        for p in range(planes):
            planes_ref[p, g * part : (g + 1) * part, :] = moved[p * part : (p + 1) * part]
    for p in range(planes):
        acc[p] = dot(planes_ref[p], weight_ref[...])
    tally(
        first_step(),
        [(acc.at[p], mask_ref.at[p], dev_ref.at[p]) for p in range(planes)],
        centre_ref,
        stats_ref,
    )


def skip_kernel(plane_ref, mask_ref, weight_ref, before_ref, dev_ref, centre_ref, stats_ref, acc, mine):
    acc[...] = dot(plane_ref[...], weight_ref[...])
    tally(first_step(), [(acc, mask_ref, dev_ref)], centre_ref, mine)
    start = before_ref.shape[1]
    stats_ref[:, :start] = before_ref[...]
    stats_ref[:, start:] = mine[...]


def mid1_kernel(
    rows_low,
    dev_in,
    centre_in,
    mask_ref,
    halo,
    halo_centre,
    halo_mask,
    stats_in,
    gain,
    shift,
    mask_out,
    weight,
    hidden,
    dev_out,
    centre_out,
    stats_out,
    taps,
    acc,
):
    low, width = acc.shape
    for lanes in lane_blocks(width):
        slope, base = affine(stats_in, gain, shift, centre_in, lanes)
        slope_edge, base_edge = affine(stats_in, gain, shift, halo_centre, lanes)

        def act(p, rows):
            mask = load_mask(mask_ref.at[p], rows)
            value = silu_half(load(dev_in.at[p], rows, lanes) * slope + base) * mask
            store(hidden.at[p], rows, lanes, value)
            return value

        def act_edge(q, i):
            rows = edge_rows(i, rows_low)
            half = load(halo.at[q], rows, lanes) * slope_edge + base_edge
            return silu_half(half) * load_mask(halo_mask.at[q], rows)

        def step(rows, i, carry):
            act(0, rows)
            store(taps.at[0], rows, lanes, shifted(act(1, rows), -1))
            store(taps.at[1], rows, lanes, from_above(act(2, rows), act_edge(0, i), rows_low))
            odd = act(3, rows)
            store(taps.at[2], rows, lanes, shifted(odd, -1))
            above = from_above(odd, act_edge(1, i), rows_low)
            store(taps.at[3], rows, lanes, above)
            store(taps.at[4], rows, lanes, shifted(above, -1))
            return carry

        sweep(low, step, 0)

    def tap(t, u):
        k = (3 * t + u) * width
        return weight[:, k : k + width]

    total = dot(hidden[0], tap(1, 1))
    total += dot(hidden[1], tap(1, 2))
    total += dot(taps[0], tap(1, 0))
    total += dot(hidden[2], tap(2, 1))
    total += dot(taps[1], tap(0, 1))
    total += dot(hidden[3], tap(2, 2))
    total += dot(taps[2], tap(2, 0))
    total += dot(taps[3], tap(0, 2))
    total += dot(taps[4], tap(0, 0))
    acc[...] = total
    tally(first_step(), [(acc, mask_out, dev_out)], centre_out, stats_out)


def expand_kernel(
    dev_in, centre_in, stats_in, gain, shift, mask, weight, hidden, dev_out, centre_out, stats_out, acc
):
    for lanes in lane_blocks(dev_in.shape[1]):
        slope, base = affine(stats_in, gain, shift, centre_in, lanes)

        def step(rows, i, carry):
            half = load(dev_in, rows, lanes) * slope + base
            store(hidden, rows, lanes, silu_half(half) * load_mask(mask, rows))
            return carry

        sweep(dev_in.shape[0], step, 0)
    acc[...] = dot(hidden[...], weight[...])
    tally(first_step(), [(acc, mask, dev_out)], centre_out, stats_out)


def join_kernel(
    dev_a,
    centre_a,
    stats_a,
    gain_a,
    shift_a,
    dev_b,
    centre_b,
    stats_b,
    gain_b,
    shift_b,
    mask,
    weight,
    first_low,
    dev_out,
    centre_out,
    stats_out,
    acc,
):
    for lanes in lane_blocks(dev_a.shape[1]):
        slope_a, base_a = affine(stats_a, gain_a, shift_a, centre_a, lanes)
        slope_b, base_b = affine(stats_b, gain_b, shift_b, centre_b, lanes)
        base = base_a + base_b

        def step(rows, i, carry):
            half = load(dev_a, rows, lanes) * slope_a + load(dev_b, rows, lanes) * slope_b + base
            store(first_low, rows, lanes, silu_half(half) * load_mask(mask, rows))
            return carry

        sweep(dev_a.shape[0], step, 0)
    acc[...] = dot(first_low[...], weight[...])
    tally(first_step(), [(acc, mask, dev_out)], centre_out, stats_out)


def mid2_kernel(
    rows_low,
    dev_in,
    centre_in,
    halo,
    halo_centre,
    halo_mask,
    stats_in,
    gain,
    shift,
    mask,
    weight,
    hidden,
    dev_out,
    centre_out,
    stats_out,
    taps,
    acc,
):
    low, width = acc.shape
    for lanes in lane_blocks(width):
        slope, base = affine(stats_in, gain, shift, centre_in, lanes)
        edges = [affine(stats_in, gain, shift, halo_centre.at[e], lanes) for e in range(2)]

        def act_edge(e, i):
            rows = edge_rows(i, rows_low)
            half = load(halo.at[e], rows, lanes) * edges[e][0] + edges[e][1]
            return silu_half(half) * load_mask(halo_mask.at[e], rows)

        def step(rows, i, carry):
            value = silu_half(load(dev_in, rows, lanes) * slope + base) * load_mask(mask, rows)
            store(hidden, rows, lanes, value)
            lines = (
                from_above(value, act_edge(0, i), rows_low),
                value,
                from_below(value, act_edge(1, i), rows_low),
            )
            for t in range(3):
                for u in range(3):
                    store(taps.at[3 * t + u], rows, lanes, shifted(lines[t], u - 1))
            return carry

        sweep(low, step, 0)
    total = dot(taps[0], weight[:, :width])
    for k in range(1, 9):
        total += dot(taps[k], weight[:, k * width : (k + 1) * width])
    acc[...] = total
    tally(first_step(), [(acc, mask, dev_out)], centre_out, stats_out)


def final_kernel(dev, centre, stats, gain, shift, first_low, cot, mask, block_out, gn_ref, sums):
    first = first_step()
    for lanes in lane_blocks(dev.shape[1]):
        slope, base = affine(stats, gain, shift, centre, lanes)

        def step(rows, i, carry):
            away = load(dev, rows, lanes)
            half = away * slope + base + 0.5 * load(first_low, rows, lanes)
            valid = load_mask(mask, rows)
            value, gate = silu_and_gate(half)
            store(block_out, rows, lanes, value * valid)
            gn = gate * valid * load(cot, rows, lanes)
            store(gn_ref, rows, lanes, gn)
            return carry[0] + column_sum(gn), carry[1] + column_sum(gn * away)

        gn_sum, gd_sum = sweep(dev.shape[0], step, (zeros8(), zeros8()))
        gn_sum, gd_sum = total_of(gn_sum), total_of(gd_sum)
        accumulate(first, sums, 0, lanes, gn_sum)
        accumulate(first, sums, 1, lanes, unit_sum(stats, centre, lanes, gn_sum, gd_sum))


def scaled(gn, away, mask, coefs):
    return (gn * coefs[0] + away * coefs[1] + coefs[2]) * mask


def gate_sums(first, grads, dev, centre, stats, gain, shift, mask, gn_ref, sums, parts):
    width = gn_ref.shape[-1]
    planes = range(parts) if parts else [None]
    for lanes in lane_blocks(width):
        slope, base = affine(stats, gain, shift, centre, lanes)
        carry = (zeros8(), zeros8())
        for p in planes:
            grad_p, dev_p, mask_p, gn_p = (
                r if p is None else r.at[p] for r in (grads, dev, mask, gn_ref)
            )

            def step(rows, i, carry, grad_p=grad_p, dev_p=dev_p, mask_p=mask_p, gn_p=gn_p):
                away = load(dev_p, rows, lanes)
                gate = gate_half(away * slope + base) * load_mask(mask_p, rows)
                gn = gate * load(grad_p, rows, lanes)
                store(gn_p, rows, lanes, gn)
                return carry[0] + column_sum(gn), carry[1] + column_sum(gn * away)

            carry = sweep(grad_p.shape[0], step, carry)
        gn_sum, gd_sum = total_of(carry[0]), total_of(carry[1])
        accumulate(first, sums, 0, lanes, gn_sum)
        accumulate(first, sums, 1, lanes, unit_sum(stats, centre, lanes, gn_sum, gd_sum))


def back_expand_kernel(
    gn,
    dev,
    centre,
    stats,
    gain,
    sums_in,
    mask,
    weight,
    dev_m,
    centre_m,
    stats_m,
    gain_m,
    shift_m,
    ga,
    gn_m,
    sums_m,
    acc,
):
    for lanes in lane_blocks(dev.shape[1]):
        coefs = back_coefs(
            stats, gain, centre, (sums_in[0:1, lanes], sums_in[1:2, lanes]), lanes
        )

        def step(rows, i, carry):
            away = load(dev, rows, lanes)
            store(ga, rows, lanes, scaled(load(gn, rows, lanes), away, load_mask(mask, rows), coefs))
            return carry

        sweep(dev.shape[0], step, 0)
    acc[...] = dot_t(ga[...], weight[...])
    gate_sums(first_step(), acc, dev_m, centre_m, stats_m, gain_m, shift_m, mask, gn_m, sums_m, 0)


def back_mid2_kernel(
    rows_low,
    gn,
    dev,
    centre,
    halo_gn,
    halo_dev,
    halo_centre,
    halo_mask,
    stats,
    gain,
    sums_in,
    mask,
    weight,
    dev_m,
    centre_m,
    stats_m,
    gain_m,
    shift_m,
    views,
    gn_m,
    sums_m,
    acc,
):
    low, width = acc.shape
    for lanes in lane_blocks(width):
        sums = (sums_in[0:1, lanes], sums_in[1:2, lanes])
        coefs = back_coefs(stats, gain, centre, sums, lanes)
        edges = [back_coefs(stats, gain, halo_centre.at[e], sums, lanes) for e in range(2)]

        def edge(e, i):
            rows = edge_rows(i, rows_low)
            return scaled(
                load(halo_gn.at[e], rows, lanes),
                load(halo_dev.at[e], rows, lanes),
                load_mask(halo_mask.at[e], rows),
                edges[e],
            )

        def step(rows, i, carry):
            value = scaled(
                load(gn, rows, lanes), load(dev, rows, lanes), load_mask(mask, rows), coefs
            )
            lines = (
                from_below(value, edge(1, i), rows_low),
                value,
                from_above(value, edge(0, i), rows_low),
            )
            for t in range(3):
                for u in range(3):
                    start = (3 * t + u) * width + lanes.start
                    store(views, rows, slice(start, start + LANES), shifted(lines[t], 1 - u))
            return carry

        sweep(low, step, 0)
    acc[...] = dot_t(views[...], weight[...])
    gate_sums(first_step(), acc, dev_m, centre_m, stats_m, gain_m, shift_m, mask, gn_m, sums_m, 0)


def back_join_kernel(
    gn_in,
    dev_in,
    centre_in,
    stats_in,
    gain_in,
    sums_in,
    mask,
    weight,
    residual,
    dev_a,
    centre_a,
    stats_a,
    gain_a,
    shift_a,
    dev_b,
    centre_b,
    stats_b,
    gain_b,
    shift_b,
    ga,
    gs_ref,
    sums,
    acc,
):
    first = first_step()
    for lanes in lane_blocks(dev_in.shape[1]):
        coefs = back_coefs(
            stats_in, gain_in, centre_in, (sums_in[0:1, lanes], sums_in[1:2, lanes]), lanes
        )

        def step(rows, i, carry):
            away = load(dev_in, rows, lanes)
            value = scaled(load(gn_in, rows, lanes), away, load_mask(mask, rows), coefs)
            store(ga, rows, lanes, value)
            return carry

        sweep(dev_in.shape[0], step, 0)
    acc[...] = dot_t(ga[...], weight[...])
    for lanes in lane_blocks(dev_a.shape[1]):
        slope_a, base_a = affine(stats_a, gain_a, shift_a, centre_a, lanes)
        slope_b, base_b = affine(stats_b, gain_b, shift_b, centre_b, lanes)
        base = base_a + base_b

        def gate(rows, i, carry):
            away_a, away_b = load(dev_a, rows, lanes), load(dev_b, rows, lanes)
            half = away_a * slope_a + away_b * slope_b + base
            grad = load(residual, rows, lanes) + load(acc, rows, lanes)
            gs = gate_half(half) * load_mask(mask, rows) * grad
            store(gs_ref, rows, lanes, gs)
            return (
                carry[0] + column_sum(gs),
                carry[1] + column_sum(gs * away_a),
                carry[2] + column_sum(gs * away_b),
            )

        carry = sweep(dev_a.shape[0], gate, (zeros8(), zeros8(), zeros8()))
        gs_sum, a_sum, b_sum = (total_of(part) for part in carry)
        accumulate(first, sums, 0, lanes, gs_sum)
        accumulate(first, sums, 1, lanes, unit_sum(stats_a, centre_a, lanes, gs_sum, a_sum))
        accumulate(first, sums, 2, lanes, unit_sum(stats_b, centre_b, lanes, gs_sum, b_sum))


def back_split_kernel(
    gs,
    dev_a,
    centre_a,
    stats_a,
    gain_a,
    dev_b,
    centre_b,
    stats_b,
    gain_b,
    sums_in,
    mask,
    weight_a,
    weight_b,
    dev_m,
    centre_m,
    stats_m,
    gain_m,
    shift_m,
    ga_a,
    ga_b,
    gn_m,
    sums_m,
    grad_skip,
    acc,
):
    for lanes in lane_blocks(dev_a.shape[1]):
        shift_sum = sums_in[0:1, lanes]
        coefs_a = back_coefs(stats_a, gain_a, centre_a, (shift_sum, sums_in[1:2, lanes]), lanes)
        coefs_b = back_coefs(stats_b, gain_b, centre_b, (shift_sum, sums_in[2:3, lanes]), lanes)

        def step(rows, i, carry):
            value, valid = load(gs, rows, lanes), load_mask(mask, rows)
            store(ga_a, rows, lanes, scaled(value, load(dev_a, rows, lanes), valid, coefs_a))
            store(ga_b, rows, lanes, scaled(value, load(dev_b, rows, lanes), valid, coefs_b))
            return carry

        sweep(dev_a.shape[0], step, 0)
    grad_skip[...] = dot_t(ga_b[...], weight_b[...]).astype(BF16)
    acc[...] = dot_t(ga_a[...], weight_a[...])
    gate_sums(first_step(), acc, dev_m, centre_m, stats_m, gain_m, shift_m, mask, gn_m, sums_m, 0)


def back_mid1_kernel(
    rows_low,
    gn,
    dev,
    centre,
    halo_gn,
    halo_dev,
    halo_centre,
    halo_mask,
    stats,
    gain,
    sums_in,
    mask,
    weight,
    dev_m,
    centre_m,
    mask_m,
    stats_m,
    gain_m,
    shift_m,
    views,
    gn_m,
    sums_m,
    acc,
):
    _, low, width = acc.shape
    for lanes in lane_blocks(width):
        sums = (sums_in[0:1, lanes], sums_in[1:2, lanes])
        coefs = back_coefs(stats, gain, centre, sums, lanes)
        coefs_edge = back_coefs(stats, gain, halo_centre, sums, lanes)

        def step(rows, i, carry):
            value = scaled(
                load(gn, rows, lanes), load(dev, rows, lanes), load_mask(mask, rows), coefs
            )
            some = edge_rows(i, rows_low)
            edge = scaled(
                load(halo_gn, some, lanes),
                load(halo_dev, some, lanes),
                load_mask(halo_mask, some),
                coefs_edge,
            )
            below = from_below(value, edge, rows_low)
            for k, view in enumerate((below, value, shifted(value, 1), shifted(below, 1))):
                start = k * width + lanes.start
                store(views, rows, slice(start, start + LANES), view)
            return carry

        sweep(low, step, 0)

    def view(k):
        return views[:, k * width : (k + 1) * width]

    def tap(t, u):
        k = (3 * t + u) * width
        return weight[:, k : k + width]

    acc[0] = dot_t(view(1), tap(1, 1))
    acc[1] = dot_t(view(1), tap(1, 2)) + dot_t(view(2), tap(1, 0))
    acc[2] = dot_t(view(1), tap(2, 1)) + dot_t(view(0), tap(0, 1))
    acc[3] = (
        dot_t(view(1), tap(2, 2))
        + dot_t(view(2), tap(2, 0))
        + dot_t(view(0), tap(0, 2))
        + dot_t(view(3), tap(0, 0))
    )
    gate_sums(
        first_step(), acc, dev_m, centre_m, stats_m, gain_m, shift_m, mask_m, gn_m, sums_m, 4
    )


def back_image_kernel(
    gn, dev, centre, stats, gain, sums_in, mask_ref, weight, grad_skip, perm_ref, ga, image, planes_ref
):
    planes, low, width = ga.shape
    for lanes in lane_blocks(width):
        coefs = back_coefs(
            stats, gain, centre, (sums_in[0:1, lanes], sums_in[1:2, lanes]), lanes
        )
        for p in range(planes):

            def step(rows, i, carry):
                away = load(dev.at[p], rows, lanes)
                valid = load_mask(mask_ref.at[p], rows)
                value = scaled(load(gn.at[p], rows, lanes), away, valid, coefs)
                store(ga.at[p], rows, lanes, value)
                return carry

            sweep(low, step, 0)
    planes_ref[0] = (dot_t(ga[0], weight[...]) + grad_skip[...].astype(F32)).astype(BF16)
    for p in range(1, planes):
        planes_ref[p] = dot_t(ga[p], weight[...]).astype(BF16)
    group = perm_ref.shape[0]
    part = group // planes
    for g in range(image.shape[0] // group):
        rows = slice(g * part, (g + 1) * part)
        mask = jnp.concatenate([mask_ref[p, rows, :] for p in range(planes)], axis=0)
        mask = jnp.concatenate([mask] * (group // 128), axis=1)
        perm = (perm_ref[...].astype(F32) * mask).astype(BF16)
        here = jnp.concatenate([planes_ref[p, rows, :] for p in range(planes)], axis=0)
        back = lax.dot_general(
            perm, here, (((0,), (0,)), ((), ())), preferred_element_type=F32
        )
        image[g * group : (g + 1) * group, :] = back.astype(BF16)


def spec_of(shape, kind, blocks):
    if kind == "rows":
        return pl.BlockSpec((shape[0] // blocks, shape[1]), lambda b: (b, 0))
    if kind == "planes":
        return pl.BlockSpec((shape[0], shape[1] // blocks, shape[2]), lambda b: (0, b, 0))
    if kind == "plane0":
        return pl.BlockSpec((None, shape[1] // blocks, shape[2]), lambda b: (0, b, 0))
    if kind == "each":
        return pl.BlockSpec((None,) + tuple(shape[1:]), lambda b: (b, 0, 0))
    if kind == "each2":
        return pl.BlockSpec((2, None) + tuple(shape[2:]), lambda b: (0, b, 0, 0))
    zero = (0,) * len(shape)
    return pl.BlockSpec(tuple(shape), lambda b: zero, pipeline_mode=pl.Buffered(1))


def out_spec(shape, kind, blocks):
    if kind == "all":
        zero = (0,) * len(shape)
        return pl.BlockSpec(tuple(shape), lambda b: zero)
    return spec_of(shape, kind, blocks)


def stage(kernel, blocks, ins, outs, scratch=(), flops=0):
    moved = sum(x.size * x.dtype.itemsize for x, _ in ins)
    moved += sum(int(np.prod(s)) * jnp.dtype(d).itemsize for s, d, _ in outs)
    return pl.pallas_call(
        kernel,
        grid=(blocks,),
        in_specs=[spec_of(x.shape, kind, blocks) for x, kind in ins],
        out_specs=[out_spec(s, kind, blocks) for s, _, kind in outs],
        out_shape=[jax.ShapeDtypeStruct(s, d) for s, d, _ in outs],
        scratch_shapes=[pltpu.VMEM(s, d) for s, d in scratch],
        compiler_params=pltpu.CompilerParams(
            dimension_semantics=("arbitrary",), vmem_limit_bytes=VMEM_BYTES
        ),
        cost_estimate=pl.CostEstimate(flops=flops, bytes_accessed=moved, transcendentals=0),
    )(*[x for x, _ in ins])


def merge_rows(buf, peers, merge, mean_only):
    if not merge:
        total = buf[0]
        for k in range(1, peers):
            total = total + buf[k]
        return total
    counts = [buf[k, 0:1, :] for k in range(peers)]
    means = [buf[k, 1:2, :] for k in range(peers)]
    count, weighted = counts[0], counts[0] * means[0]
    for k in range(1, peers):
        count = count + counts[k]
        weighted = weighted + counts[k] * means[k]
    safe = jnp.maximum(count, 1.0)
    mean = weighted / safe
    squares = jnp.zeros_like(mean)
    for k in range(peers):
        squares = squares + buf[k, 2:3, :] + counts[k] * jnp.square(means[k] - mean)
    if mean_only:
        squares = squares / safe
    return jnp.concatenate([count, mean, squares], axis=0)


def sync_kernel(rows_n, img_n, merge, widths, mine, *refs):
    outs = refs[: len(widths)]
    buf_r, buf_i, part, send_r, recv_r, send_i, recv_i = refs[len(widths) :]
    row, img = lax.axis_index("rows"), lax.axis_index("img")
    barrier = pltpu.get_barrier_semaphore()
    for k in range(1, rows_n):
        peer = lax.rem(row + k, rows_n)
        pl.semaphore_signal(barrier, inc=1, device_id={"rows": peer}, device_id_type=MESH)
    for k in range(1, img_n):
        peer = lax.rem(img + k, img_n)
        pl.semaphore_signal(barrier, inc=1, device_id={"img": peer}, device_id_type=MESH)
    pl.semaphore_wait(barrier, rows_n + img_n - 2)
    copies = []

    def exchange(axis, me, peers, source, buf, send, recv):
        for k in range(1, peers):
            copy = pltpu.make_async_remote_copy(
                src_ref=source,
                dst_ref=buf.at[me],
                send_sem=send.at[k],
                recv_sem=recv.at[me],
                device_id={axis: lax.rem(me + k, peers)},
                device_id_type=MESH,
            )
            copy.start()
            copies.append(copy)
        buf[pl.ds(me, 1)] = source[...][None]
        for k in range(1, peers):
            peer = lax.rem(me + k, peers)
            pltpu.make_async_remote_copy(
                src_ref=source,
                dst_ref=buf.at[peer],
                send_sem=send.at[k],
                recv_sem=recv.at[peer],
                device_id={axis: peer},
                device_id_type=MESH,
            ).wait_recv()

    exchange("rows", row, rows_n, mine, buf_r, send_r, recv_r)
    part[...] = merge_rows(buf_r, rows_n, merge, False)
    exchange("img", img, img_n, part, buf_i, send_i, recv_i)
    total = merge_rows(buf_i, img_n, merge, True)
    start = 0
    for out, width in zip(outs, widths):
        out[...] = total[:, start : start + width]
        start += width
    for copy in copies:
        copy.wait_send()


class Sync:
    def __init__(self, rows_n, img_n):
        self.rows_n, self.img_n = rows_n, img_n
        self.ids = {}

    def __call__(self, mine, merge, widths=None):
        lines, width = mine.shape
        widths = widths or (width,)
        key = (merge, lines, tuple(widths))
        ident = self.ids.setdefault(key, len(self.ids))
        shape = (lines, width)
        dma = pltpu.SemaphoreType.DMA
        out = pl.pallas_call(
            functools.partial(sync_kernel, self.rows_n, self.img_n, merge, widths),
            in_specs=[pl.BlockSpec(memory_space=pltpu.VMEM)],
            out_specs=[pl.BlockSpec(memory_space=pltpu.VMEM)] * len(widths),
            out_shape=[jax.ShapeDtypeStruct((lines, w), F32) for w in widths],
            scratch_shapes=[
                pltpu.VMEM((self.rows_n,) + shape, F32),
                pltpu.VMEM((self.img_n,) + shape, F32),
                pltpu.VMEM(shape, F32),
                dma((self.rows_n,)),
                dma((self.rows_n,)),
                dma((self.img_n,)),
                dma((self.img_n,)),
            ],
            compiler_params=pltpu.CompilerParams(collective_id=ident, has_side_effects=True),
            cost_estimate=pl.CostEstimate(
                flops=12_000_000_000, bytes_accessed=1_000_000, transcendentals=0
            ),
        )(mine)
        return out[0] if len(widths) == 1 else out


def to_next(x, peers):
    return lax.ppermute(x, "rows", [(i, i + 1) for i in range(peers - 1)])


def to_previous(x, peers):
    return lax.ppermute(x, "rows", [(i + 1, i) for i in range(peers - 1)])


def lanes128(mask):
    return jnp.broadcast_to(mask.astype(F32)[..., None], mask.shape + (128,))


def body(
    image_in,
    extent,
    weight_in1,
    weight_mid1,
    weight_out1,
    weight_skip,
    weight_in2,
    weight_mid2,
    weight_out2,
    gain_in1,
    shift_in1,
    gain_mid1,
    shift_mid1,
    gain_out1,
    shift_out1,
    gain_skip,
    shift_skip,
    gain_in2,
    shift_in2,
    gain_mid2,
    shift_mid2,
    gain_out2,
    shift_out2,
    cotangent,
):
    images, rows_here, columns, inputs = image_in.shape
    middle, outputs = weight_out1.shape
    rows_low, cols_low = rows_here // 2, columns // 2
    low = images * rows_low * cols_low
    rows_n, img_n = lax.axis_size("rows"), lax.axis_size("img")
    blocks = images // IMAGES
    per_block = low // blocks
    edge = images * cols_low
    sync = Sync(rows_n, img_n)
    run = functools.partial(stage, blocks=blocks)

    row0 = lax.axis_index("rows") * rows_here
    half = extent // 2

    def inside(rows, cols, side):
        kept = (rows[None, :, None] >= 0) & (rows[None, :, None] < side[:, None, None])
        return kept & (cols[None, None, :] < side[:, None, None])

    low_rows = jnp.arange(rows_low, dtype=jnp.int32)
    low_cols = jnp.arange(cols_low, dtype=jnp.int32)
    mask_in = jnp.stack(
        [
            inside(row0 + 2 * low_rows + p, 2 * low_cols + q, extent).reshape(-1)
            for p in range(2)
            for q in range(2)
        ]
    )
    mask_in = lanes128(mask_in)
    mask_out = lanes128(inside(row0 // 2 + low_rows, low_cols, half).reshape(-1))
    above = jnp.stack([row0 - 1])
    mask_above = lanes128(
        jnp.stack([inside(above, 2 * low_cols + q, extent).reshape(-1) for q in range(2)])
    )
    mask_edges = lanes128(
        jnp.stack(
            [
                inside(jnp.stack([line]), low_cols, half).reshape(-1)
                for line in (row0 // 2 - 1, row0 // 2 + rows_low)
            ]
        )
    )

    group_images = 256 // (rows_here * columns)
    order = np.arange(256).reshape(group_images, rows_low, 2, cols_low, 2)
    order = order.transpose(2, 4, 0, 1, 3).reshape(-1)
    perm = jnp.asarray(np.eye(256, dtype=np.float32)[order], BF16)

    def row(vector):
        return vector.reshape(1, -1)

    g_in1, s_in1, g_mid1, s_mid1 = row(gain_in1), row(shift_in1), row(gain_mid1), row(shift_mid1)
    g_out1, s_out1, g_skip, s_skip = row(gain_out1), row(shift_out1), row(gain_skip), row(shift_skip)
    g_in2, s_in2, g_mid2, s_mid2 = row(gain_in2), row(shift_in2), row(gain_mid2), row(shift_mid2)
    g_out2, s_out2 = row(gain_out2), row(shift_out2)
    kernel_mid1 = weight_mid1.reshape(middle, 9 * middle)
    kernel_mid2 = weight_mid2.reshape(middle, 9 * middle)
    cot = cotangent.reshape(low, outputs)

    dev_mid_out = [
        ((low, middle), BF16, "rows"),
        ((blocks, 1, middle), F32, "each"),
        ((3, middle), F32, "all"),
    ]
    dev_out_out = [
        ((low, outputs), BF16, "rows"),
        ((blocks, 1, outputs), F32, "each"),
        ((3, outputs), F32, "all"),
    ]
    unit_flops = 2 * low * middle * middle

    planes, d_in1, c_in1, t_in1 = run(
        split_kernel,
        ins=[
            (image_in.reshape(4 * low, inputs), "rows"),
            (perm, "all"),
            (mask_in, "planes"),
            (weight_in1, "all"),
        ],
        outs=[
            ((4, low, inputs), BF16, "planes"),
            ((4, low, middle), BF16, "planes"),
            ((blocks, 1, middle), F32, "each"),
            ((3, middle), F32, "all"),
        ],
        scratch=[((4, per_block, middle), F32)],
        flops=12 * unit_flops,
    )
    last = d_in1.reshape(2, 2, images, rows_low, cols_low, middle)[1, :, :, rows_low - 1]
    halo_in1 = to_next(last.reshape(2, edge, middle), rows_n)
    halo_c_in1 = to_next(c_in1, rows_n)
    d_skip, c_skip, t_in1 = run(
        skip_kernel,
        ins=[(planes, "plane0"), (mask_out, "rows"), (weight_skip, "all"), (t_in1, "all")],
        outs=dev_out_out[:2] + [((3, middle + outputs), F32, "all")],
        scratch=[((per_block, outputs), F32), ((3, outputs), F32)],
        flops=8 * unit_flops,
    )
    n_in1, n_skip = sync(t_in1, True, (middle, outputs))
    hid_in1, d_mid1, c_mid1, t_mid1 = run(
        functools.partial(mid1_kernel, rows_low),
        ins=[
            (d_in1, "planes"),
            (c_in1, "each"),
            (mask_in, "planes"),
            (halo_in1, "planes"),
            (halo_c_in1, "each"),
            (mask_above, "planes"),
            (n_in1, "all"),
            (g_in1, "all"),
            (s_in1, "all"),
            (mask_out, "rows"),
            (kernel_mid1, "all"),
        ],
        outs=[((4, low, middle), BF16, "planes")] + dev_mid_out,
        scratch=[((5, per_block, middle), BF16), ((per_block, middle), F32)],
        flops=9 * unit_flops,
    )
    n_mid1 = sync(t_mid1, True)
    image_mid1 = d_mid1.reshape(images, rows_low, cols_low, middle)
    halo_mid1 = to_previous(image_mid1[:, 0].reshape(edge, middle), rows_n)
    halo_c_mid1 = to_previous(c_mid1, rows_n)
    hid_mid1, d_out1, c_out1, t_out1 = run(
        expand_kernel,
        ins=[
            (d_mid1, "rows"),
            (c_mid1, "each"),
            (n_mid1, "all"),
            (g_mid1, "all"),
            (s_mid1, "all"),
            (mask_out, "rows"),
            (weight_out1, "all"),
        ],
        outs=[((low, middle), BF16, "rows")] + dev_out_out,
        scratch=[((per_block, outputs), F32)],
        flops=4 * unit_flops,
    )
    n_out1 = sync(t_out1, True)
    join = [
        (d_out1, "rows"),
        (c_out1, "each"),
        (n_out1, "all"),
        (g_out1, "all"),
        (s_out1, "all"),
        (d_skip, "rows"),
        (c_skip, "each"),
        (n_skip, "all"),
        (g_skip, "all"),
        (s_skip, "all"),
    ]
    first_low, d_in2, c_in2, t_in2 = run(
        join_kernel,
        ins=join + [(mask_out, "rows"), (weight_in2, "all")],
        outs=[((low, outputs), BF16, "rows")] + dev_mid_out,
        scratch=[((per_block, middle), F32)],
        flops=4 * unit_flops,
    )

    def edges_of(x):
        image = x.reshape(images, rows_low, cols_low, middle)
        return jnp.stack(
            [
                to_next(image[:, rows_low - 1].reshape(edge, middle), rows_n),
                to_previous(image[:, 0].reshape(edge, middle), rows_n),
            ]
        )

    def centres_of(c):
        return jnp.stack([to_next(c, rows_n), to_previous(c, rows_n)])

    halo_in2, halo_c_in2 = edges_of(d_in2), centres_of(c_in2)
    n_in2 = sync(t_in2, True)
    hid_in2, d_mid2, c_mid2, t_mid2 = run(
        functools.partial(mid2_kernel, rows_low),
        ins=[
            (d_in2, "rows"),
            (c_in2, "each"),
            (halo_in2, "planes"),
            (halo_c_in2, "each2"),
            (mask_edges, "planes"),
            (n_in2, "all"),
            (g_in2, "all"),
            (s_in2, "all"),
            (mask_out, "rows"),
            (kernel_mid2, "all"),
        ],
        outs=[((low, middle), BF16, "rows")] + dev_mid_out,
        scratch=[((9, per_block, middle), BF16), ((per_block, middle), F32)],
        flops=9 * unit_flops,
    )
    n_mid2 = sync(t_mid2, True)
    halo_mid2, halo_c_mid2 = edges_of(d_mid2), centres_of(c_mid2)
    hid_mid2, d_out2, c_out2, t_out2 = run(
        expand_kernel,
        ins=[
            (d_mid2, "rows"),
            (c_mid2, "each"),
            (n_mid2, "all"),
            (g_mid2, "all"),
            (s_mid2, "all"),
            (mask_out, "rows"),
            (weight_out2, "all"),
        ],
        outs=[((low, middle), BF16, "rows")] + dev_out_out,
        scratch=[((per_block, outputs), F32)],
        flops=4 * unit_flops,
    )
    n_out2 = sync(t_out2, True)
    block_out, gn_out2, z_out2 = run(
        final_kernel,
        ins=[
            (d_out2, "rows"),
            (c_out2, "each"),
            (n_out2, "all"),
            (g_out2, "all"),
            (s_out2, "all"),
            (first_low, "rows"),
            (cot, "rows"),
            (mask_out, "rows"),
        ],
        outs=[
            ((low, outputs), BF16, "rows"),
            ((low, outputs), BF16, "rows"),
            ((2, outputs), F32, "all"),
        ],
    )

    z_out2 = sync(z_out2, False)
    gn_mid_out = [((low, middle), BF16, "rows"), ((2, middle), F32, "all")]
    ga_out2, gn_mid2, z_mid2 = run(
        back_expand_kernel,
        ins=[
            (gn_out2, "rows"),
            (d_out2, "rows"),
            (c_out2, "each"),
            (n_out2, "all"),
            (g_out2, "all"),
            (z_out2, "all"),
            (mask_out, "rows"),
            (weight_out2, "all"),
            (d_mid2, "rows"),
            (c_mid2, "each"),
            (n_mid2, "all"),
            (g_mid2, "all"),
            (s_mid2, "all"),
        ],
        outs=[((low, outputs), BF16, "rows")] + gn_mid_out,
        scratch=[((per_block, middle), F32)],
        flops=4 * unit_flops,
    )
    halo_gn_mid2 = edges_of(gn_mid2)
    z_mid2 = sync(z_mid2, False)
    views2, gn_in2, z_in2 = run(
        functools.partial(back_mid2_kernel, rows_low),
        ins=[
            (gn_mid2, "rows"),
            (d_mid2, "rows"),
            (c_mid2, "each"),
            (halo_gn_mid2, "planes"),
            (halo_mid2, "planes"),
            (halo_c_mid2, "each2"),
            (mask_edges, "planes"),
            (n_mid2, "all"),
            (g_mid2, "all"),
            (z_mid2, "all"),
            (mask_out, "rows"),
            (kernel_mid2, "all"),
            (d_in2, "rows"),
            (c_in2, "each"),
            (n_in2, "all"),
            (g_in2, "all"),
            (s_in2, "all"),
        ],
        outs=[((low, 9 * middle), BF16, "rows")] + gn_mid_out,
        scratch=[((per_block, middle), F32)],
        flops=9 * unit_flops,
    )
    z_in2 = sync(z_in2, False)
    ga_in2, gs1, z_sum1 = run(
        back_join_kernel,
        ins=[
            (gn_in2, "rows"),
            (d_in2, "rows"),
            (c_in2, "each"),
            (n_in2, "all"),
            (g_in2, "all"),
            (z_in2, "all"),
            (mask_out, "rows"),
            (weight_in2, "all"),
            (gn_out2, "rows"),
        ]
        + join,
        outs=[
            ((low, middle), BF16, "rows"),
            ((low, outputs), BF16, "rows"),
            ((3, outputs), F32, "all"),
        ],
        scratch=[((per_block, outputs), F32)],
        flops=4 * unit_flops,
    )

    z_sum1 = sync(z_sum1, False)
    ga_out1, ga_skip, gn_mid1, z_mid1, grad_skip_in = run(
        back_split_kernel,
        ins=[
            (gs1, "rows"),
            (d_out1, "rows"),
            (c_out1, "each"),
            (n_out1, "all"),
            (g_out1, "all"),
            (d_skip, "rows"),
            (c_skip, "each"),
            (n_skip, "all"),
            (g_skip, "all"),
            (z_sum1, "all"),
            (mask_out, "rows"),
            (weight_out1, "all"),
            (weight_skip, "all"),
            (d_mid1, "rows"),
            (c_mid1, "each"),
            (n_mid1, "all"),
            (g_mid1, "all"),
            (s_mid1, "all"),
        ],
        outs=[((low, outputs), BF16, "rows"), ((low, outputs), BF16, "rows")]
        + gn_mid_out
        + [((low, inputs), BF16, "rows")],
        scratch=[((per_block, middle), F32)],
        flops=12 * unit_flops,
    )
    first_rows = gn_mid1.reshape(images, rows_low, cols_low, middle)[:, 0]
    halo_gn_mid1 = to_previous(first_rows.reshape(edge, middle), rows_n)
    z_mid1 = sync(z_mid1, False)
    views1, gn_in1, z_in1 = run(
        functools.partial(back_mid1_kernel, rows_low),
        ins=[
            (gn_mid1, "rows"),
            (d_mid1, "rows"),
            (c_mid1, "each"),
            (halo_gn_mid1, "rows"),
            (halo_mid1, "rows"),
            (halo_c_mid1, "each"),
            (mask_edges[1], "rows"),
            (n_mid1, "all"),
            (g_mid1, "all"),
            (z_mid1, "all"),
            (mask_out, "rows"),
            (kernel_mid1, "all"),
            (d_in1, "planes"),
            (c_in1, "each"),
            (mask_in, "planes"),
            (n_in1, "all"),
            (g_in1, "all"),
            (s_in1, "all"),
        ],
        outs=[
            ((low, 4 * middle), BF16, "rows"),
            ((4, low, middle), BF16, "planes"),
            ((2, middle), F32, "all"),
        ],
        scratch=[((4, per_block, middle), F32)],
        flops=9 * unit_flops,
    )
    z_in1 = sync(z_in1, False)
    ga_in1, grad_image = run(
        back_image_kernel,
        ins=[
            (gn_in1, "planes"),
            (d_in1, "planes"),
            (c_in1, "each"),
            (n_in1, "all"),
            (g_in1, "all"),
            (z_in1, "all"),
            (mask_in, "planes"),
            (weight_in1, "all"),
            (grad_skip_in, "rows"),
            (perm, "all"),
        ],
        outs=[((4, low, middle), BF16, "planes"), ((4 * low, inputs), BF16, "rows")],
        scratch=[((4, per_block, inputs), BF16)],
        flops=12 * unit_flops,
    )

    def weight_term(values, upstream):
        return lax.dot_general(
            values, upstream, (((0,), (0,)), ((), ())), preferred_element_type=F32
        ).astype(BF16)

    def reduced(grad):
        shard = lax.psum_scatter(grad, "img", scatter_dimension=0, tiled=True)
        return lax.psum(shard, "rows").astype(F32)

    dw_out2 = reduced(weight_term(hid_mid2, ga_out2))
    dw_mid2 = reduced(weight_term(hid_in2, views2))
    dw_in2 = reduced(weight_term(first_low, ga_in2))
    dw_out1 = reduced(weight_term(hid_mid1, ga_out1))
    dw_skip = reduced(weight_term(planes[0], ga_skip))
    m = middle
    dw_00 = weight_term(hid_in1[0], views1[:, m : 2 * m])
    dw_01 = weight_term(hid_in1[1], views1[:, m : 3 * m])
    dw_10 = weight_term(hid_in1[2], views1[:, : 2 * m])
    dw_11 = weight_term(hid_in1[3], views1)
    dw_mid1 = jnp.concatenate(
        [
            dw_11[:, 3 * m :],
            dw_10[:, :m],
            dw_11[:, :m],
            dw_01[:, m:],
            dw_00,
            dw_01[:, :m],
            dw_11[:, 2 * m : 3 * m],
            dw_10[:, m:],
            dw_11[:, m : 2 * m],
        ],
        axis=1,
    )
    dw_mid1 = reduced(dw_mid1)
    dw_in1 = reduced(
        weight_term(planes.reshape(4 * low, inputs), ga_in1.reshape(4 * low, middle))
    )
    kernel_shape = (middle // img_n, 3, 3, middle)
    return (
        block_out.reshape(images, rows_low, cols_low, outputs),
        grad_image.reshape(images, rows_here, columns, inputs),
        dw_in1,
        dw_mid1.reshape(kernel_shape),
        dw_out1,
        dw_skip,
        dw_in2,
        dw_mid2.reshape(kernel_shape),
        dw_out2,
        z_in1[1],
        z_in1[0],
        z_mid1[1],
        z_mid1[0],
        z_sum1[1],
        z_sum1[0],
        z_sum1[2],
        z_sum1[0],
        z_in2[1],
        z_in2[0],
        z_mid2[1],
        z_mid2[0],
        z_out2[1],
        z_out2[0],
    )


def solution(mesh):
    image = P("img", "rows", None, None)
    in_specs = (image, P("img")) + (P(),) * 21 + (image,)
    out_specs = (
        image,
        image,
        P("img", None),
        P("img", None, None, None),
        P("img", None),
        P("img", None),
        P("img", None),
        P("img", None, None, None),
        P("img", None),
    ) + (P(),) * 14
    return jax.shard_map(body, mesh=mesh, in_specs=in_specs, out_specs=out_specs, check_vma=False)
```

profile of v0, /device:TPU:0, one launch (start us, length us, event | category | flops | bytes accessed | tf_op | source)
XLA Modules:
  0.0 934.8 jit_solution(6244088292835012623)
XLA Ops:
  11.8 17.4 %shard_map.416 = (bf16[4,1280,1024]{2,1,0:T(8,128)(2,1)}, bf16[4,1280,512]{2,1,0:T(8,128)(2,1)}, f32[5,1,512]{2,1,0:T(1,128)}, f32[3,512]{1,0:T(4,128)}) custom-call(bf16[5120,1024]{1,0:T(8,128)(2,1)} %bitcast.191, bf16[256,256]{1,0:T(8,128)(2,1)} %constant.48.clone.perm_ref, f32[4,1280,128]{2,1,0:T(8,128)} %broadcast_in_dim.14.mask_ref.mask_m, ...), custom_call_target="tpu_custom_call" | custom-call | flops 8053063680 | bytes 30031872 | tf_op jit(solution)/shard_map/pallas_call | solution.py:769
  42.5 14.6 %shard_map.417 = (bf16[1280,2048]{1,0:T(8,128)(2,1)}, f32[5,1,2048]{2,1,0:T(1,128)}, f32[3,2560]{1,0:T(4,128)}) custom-call(bf16[4,1280,1024]{2,1,0:T(8,128)(2,1)} %get-tuple-element.76.plane_ref, f32[1280,128]{1,0:T(8,128)} %broadcast_in_dim.16.mask_ref.mask_out.mask, bf16[1024,2048]{1,0:T(8,128)(2,1)} %weight_b.1, f32[3,512]{1,0:T(4,128)} %get-tuple-element.77.before_ref), custom_call_target="tpu_custom_call" | custom-call | flops 5368709120 | bytes 20656128 | tf_op jit(solution)/shard_map/pallas_call | solution.py:769
  57.1 13.1 %shard_map.418 = (f32[3,512]{1,0:T(4,128)}, f32[3,2048]{1,0:T(4,128)}) custom-call(f32[3,2560]{1,0:T(4,128)} %get-tuple-element.78.mine), custom_call_target="tpu_custom_call" | custom-call | flops 12000000000 | bytes 1000000 | tf_op jit(solution)/shard_map/pallas_call | solution.py:867
  98.6 16.7 %shard_map.419 = (bf16[4,1280,512]{2,1,0:T(8,128)(2,1)}, bf16[1280,512]{1,0:T(8,128)(2,1)}, f32[5,1,512]{2,1,0:T(1,128)}, f32[3,512]{1,0:T(4,128)}) custom-call(bf16[4,1280,512]{2,1,0:T(8,128)(2,1)} %get-tuple-element.74.dev_in.dev_m.dev, f32[5,1,512]{2,1,0:T(1,128)} %get-tuple-element.75.centre_in.centre_m.centre, ...), custom_call_target="tpu_custom_call" | custom-call | flops 6039797760 | bytes 21805056 | tf_op jit(solution)/shard_map/pallas_call | solution.py:769
  115.4 17.8 %shard_map.420.stats_in.stats_m.stats = f32[3,512]{1,0:T(4,128)} custom-call(f32[3,512]{1,0:T(4,128)} %get-tuple-element.82.mine), custom_call_target="tpu_custom_call" | custom-call | flops 12000000000 | bytes 1000000 | tf_op jit(solution)/shard_map/pallas_call | solution.py:867
  133.1 12.4 %shard_map.421 = (bf16[1280,512]{1,0:T(8,128)(2,1)}, bf16[1280,2048]{1,0:T(8,128)(2,1)}, f32[5,1,2048]{2,1,0:T(1,128)}, f32[3,2048]{1,0:T(4,128)}) custom-call(bf16[1280,512]{1,0:T(8,128)(2,1)} %get-tuple-element.80.dev_in.dev_m.dev, f32[5,1,512]{2,1,0:T(1,128)} %get-tuple-element.81.centre_in.centre_m.centre, f32[3,512]{1,0:T(4,128)} %shard_map.420.stats_in.stats_m.stats, ...), custom_call_target="tpu_custom_call" | custom-call | flops 2684354560 | bytes 10702848 | tf_op jit(solution)/shard_map/pallas_call | solution.py:769
  145.6 11.9 %shard_map.422.stats_a = f32[3,2048]{1,0:T(4,128)} custom-call(f32[3,2048]{1,0:T(4,128)} %get-tuple-element.85.mine), custom_call_target="tpu_custom_call" | custom-call | flops 12000000000 | bytes 1000000 | tf_op jit(solution)/shard_map/pallas_call | solution.py:867
  157.5 14.2 %shard_map.423 = (bf16[1280,2048]{1,0:T(8,128)(2,1)}, bf16[1280,512]{1,0:T(8,128)(2,1)}, f32[5,1,512]{2,1,0:T(1,128)}, f32[3,512]{1,0:T(4,128)}) custom-call(bf16[1280,2048]{1,0:T(8,128)(2,1)} %get-tuple-element.83.dev_a, f32[5,1,2048]{2,1,0:T(1,128)} %get-tuple-element.84.centre_a, f32[3,2048]{1,0:T(4,128)} %shard_map.422.stats_a, f32[1,2048]{1,0:T(1,128)} %bitcast.158, ...), custom_call_target="tpu_custom_call" | custom-call | flops 2684354560 | bytes 19972096 | tf_op jit(solution)/shard_map/pallas_call | solution.py:769
  183.5 21.5 %shard_map.424.stats_in.stats_m = f32[3,512]{1,0:T(4,128)} custom-call(f32[3,512]{1,0:T(4,128)} %get-tuple-element.91.mine), custom_call_target="tpu_custom_call" | custom-call | flops 12000000000 | bytes 1000000 | tf_op jit(solution)/shard_map/pallas_call | solution.py:867
  209.9 14.4 %shard_map.425 = (bf16[1280,512]{1,0:T(8,128)(2,1)}, bf16[1280,512]{1,0:T(8,128)(2,1)}, f32[5,1,512]{2,1,0:T(1,128)}, f32[3,512]{1,0:T(4,128)}) custom-call(bf16[1280,512]{1,0:T(8,128)(2,1)} %get-tuple-element.89.dev_in.dev_m, f32[5,1,512]{2,1,0:T(1,128)} %get-tuple-element.90.centre_in.centre_m, bf16[2,640,512]{2,1,0:T(8,128)(2,1)} %pad_maximum_fusion.halo, ...), custom_call_target="tpu_custom_call" | custom-call | flops 6039797760 | bytes 11329536 | tf_op jit(solution)/shard_map/pallas_call | solution.py:769
  244.6 12.4 %shard_map.427 = (bf16[1280,512]{1,0:T(8,128)(2,1)}, bf16[1280,2048]{1,0:T(8,128)(2,1)}, f32[5,1,2048]{2,1,0:T(1,128)}, f32[3,2048]{1,0:T(4,128)}) custom-call(bf16[1280,512]{1,0:T(8,128)(2,1)} %get-tuple-element.92.dev_in.dev_m.dev, f32[5,1,512]{2,1,0:T(1,128)} %get-tuple-element.93.centre_in.centre_m.centre, f32[3,512]{1,0:T(4,128)} %shard_map.426.stats_in.stats_m.stats, ...), custom_call_target="tpu_custom_call" | custom-call | flops 2684354560 | bytes 10702848 | tf_op jit(solution)/shard_map/pallas_call | solution.py:769
  257.0 13.2 %shard_map.428.stats = f32[3,2048]{1,0:T(4,128)} custom-call(f32[3,2048]{1,0:T(4,128)} %get-tuple-element.97.mine), custom_call_target="tpu_custom_call" | custom-call | flops 12000000000 | bytes 1000000 | tf_op jit(solution)/shard_map/pallas_call | solution.py:867
  270.2 14.5 %shard_map.429 = (bf16[1280,2048]{1,0:T(8,128)(2,1)}, bf16[1280,2048]{1,0:T(8,128)(2,1)}, f32[2,2048]{1,0:T(2,128)}) custom-call(bf16[1280,2048]{1,0:T(8,128)(2,1)} %get-tuple-element.95.dev, f32[5,1,2048]{2,1,0:T(1,128)} %get-tuple-element.96.centre, f32[3,2048]{1,0:T(4,128)} %shard_map.428.stats, f32[1,2048]{1,0:T(1,128)} %bitcast.152, ...), custom_call_target="tpu_custom_call" | custom-call | bytes 26968064 | tf_op jit(solution)/shard_map/pallas_call | solution.py:769
  284.7 11.5 %shard_map.430.sums_in = f32[2,2048]{1,0:T(2,128)} custom-call(f32[2,2048]{1,0:T(2,128)} %get-tuple-element.101.mine), custom_call_target="tpu_custom_call" | custom-call | flops 12000000000 | bytes 1000000 | tf_op jit(solution)/shard_map/pallas_call | solution.py:867
  296.2 13.6 %shard_map.431 = (bf16[1280,2048]{1,0:T(8,128)(2,1)}, bf16[1280,512]{1,0:T(8,128)(2,1)}, f32[2,512]{1,0:T(2,128)}) custom-call(bf16[1280,2048]{1,0:T(8,128)(2,1)} %get-tuple-element.100.gn.residual, bf16[1280,2048]{1,0:T(8,128)(2,1)} %get-tuple-element.95.dev, f32[5,1,2048]{2,1,0:T(1,128)} %get-tuple-element.96.centre, f32[3,2048]{1,0:T(4,128)} %shard_map.428.stats, ...), custom_call_target="tpu_custom_call" | custom-call | flops 2684354560 | bytes 21217280 | tf_op jit(solution)/shard_map/pallas_call | solution.py:769
  316.3 23.1 %shard_map.432.sums_in = f32[2,512]{1,0:T(2,128)} custom-call(f32[2,512]{1,0:T(2,128)} %get-tuple-element.103.mine), custom_call_target="tpu_custom_call" | custom-call | flops 12000000000 | bytes 1000000 | tf_op jit(solution)/shard_map/pallas_call | solution.py:867
  346.1 16.0 %shard_map.433 = (bf16[1280,4608]{1,0:T(8,128)(2,1)}, bf16[1280,512]{1,0:T(8,128)(2,1)}, f32[2,512]{1,0:T(2,128)}) custom-call(bf16[1280,512]{1,0:T(8,128)(2,1)} %get-tuple-element.102.gn, bf16[1280,512]{1,0:T(8,128)(2,1)} %get-tuple-element.92.dev_in.dev_m.dev, f32[5,1,512]{2,1,0:T(1,128)} %get-tuple-element.93.centre_in.centre_m.centre, ...), custom_call_target="tpu_custom_call" | custom-call | flops 6039797760 | bytes 25757696 | tf_op jit(solution)/shard_map/pallas_call | solution.py:769
  362.1 12.7 %shard_map.434.sums_in = f32[2,512]{1,0:T(2,128)} custom-call(f32[2,512]{1,0:T(2,128)} %get-tuple-element.105.mine), custom_call_target="tpu_custom_call" | custom-call | flops 12000000000 | bytes 1000000 | tf_op jit(solution)/shard_map/pallas_call | solution.py:867
  374.8 12.3 %convolution_convert_fusion = bf16[512,4608]{1,0:T(8,128)(2,1)} fusion(bf16[1280,512]{1,0:T(8,128)(2,1)S(1)} %copy-done.21, bf16[1280,4608]{1,0:T(8,128)(2,1)} %get-tuple-element.122), kind=kOutput, calls=%fused_computation | convolution fusion | flops 6042157056 | bytes 17825792 | tf_op jit(solution)/shard_map/dot_general | solution.py:1310
  387.5 20.1 %shard_map.435 = (bf16[1280,512]{1,0:T(8,128)(2,1)}, bf16[1280,2048]{1,0:T(8,128)(2,1)}, f32[3,2048]{1,0:T(4,128)}) custom-call(bf16[1280,512]{1,0:T(8,128)(2,1)} %get-tuple-element.104.gn_in, bf16[1280,512]{1,0:T(8,128)(2,1)} %get-tuple-element.89.dev_in.dev_m, f32[5,1,512]{2,1,0:T(1,128)} %get-tuple-element.90.centre_in.centre_m, ...), custom_call_target="tpu_custom_call" | custom-call | flops 2684354560 | bytes 27867136 | tf_op jit(solution)/shard_map/pallas_call | solution.py:769
  407.5 14.5 %shard_map.436.sums_in = f32[3,2048]{1,0:T(4,128)} custom-call(f32[3,2048]{1,0:T(4,128)} %get-tuple-element.107.mine), custom_call_target="tpu_custom_call" | custom-call | flops 12000000000 | bytes 1000000 | tf_op jit(solution)/shard_map/pallas_call | solution.py:867
  422.0 23.8 %shard_map.437 = (bf16[1280,2048]{1,0:T(8,128)(2,1)}, bf16[1280,2048]{1,0:T(8,128)(2,1)}, bf16[1280,512]{1,0:T(8,128)(2,1)}, f32[2,512]{1,0:T(2,128)}, bf16[1280,1024]{1,0:T(8,128)(2,1)}) custom-call(bf16[1280,2048]{1,0:T(8,128)(2,1)} %get-tuple-element.106.gs, bf16[1280,2048]{1,0:T(8,128)(2,1)} %get-tuple-element.83.dev_a, ...), custom_call_target="tpu_custom_call" | custom-call | flops 8053063680 | bytes 38600704 | tf_op jit(solution)/shard_map/pallas_call | solution.py:769
  448.3 23.8 %shard_map.438.sums_in = f32[2,512]{1,0:T(2,128)} custom-call(f32[2,512]{1,0:T(2,128)} %get-tuple-element.109.mine), custom_call_target="tpu_custom_call" | custom-call | flops 12000000000 | bytes 1000000 | tf_op jit(solution)/shard_map/pallas_call | solution.py:867
  473.3 20.6 %shard_map.439 = (bf16[1280,2048]{1,0:T(8,128)(2,1)}, bf16[4,1280,512]{2,1,0:T(8,128)(2,1)}, f32[2,512]{1,0:T(2,128)}) custom-call(bf16[1280,512]{1,0:T(8,128)(2,1)} %get-tuple-element.108.gn, bf16[1280,512]{1,0:T(8,128)(2,1)} %get-tuple-element.80.dev_in.dev_m.dev, f32[5,1,512]{2,1,0:T(1,128)} %get-tuple-element.81.centre_in.centre_m.centre, ...), custom_call_target="tpu_custom_call" | custom-call | flops 6039797760 | bytes 28041216 | tf_op jit(solution)/shard_map/pallas_call | solution.py:769
  523.2 18.1 %shard_map.441 = (bf16[4,1280,512]{2,1,0:T(8,128)(2,1)}, bf16[5120,1024]{1,0:T(8,128)(2,1)}) custom-call(bf16[4,1280,512]{2,1,0:T(8,128)(2,1)} %get-tuple-element.110.gn, bf16[4,1280,512]{2,1,0:T(8,128)(2,1)} %get-tuple-element.74.dev_in.dev_m.dev, f32[5,1,512]{2,1,0:T(1,128)} %get-tuple-element.75.centre_in.centre_m.centre, ...), custom_call_target="tpu_custom_call" | custom-call | flops 8053063680 | bytes 32659456 | tf_op jit(solution)/shard_map/pallas_call | solution.py:769
  541.3 10.8 %bitcast_convert_fusion = bf16[1024,512]{1,0:T(8,128)(2,1)} fusion(bf16[4,1280,1024]{2,1,0:T(8,128)(2,1)} %get-tuple-element.76.plane_ref, bf16[4,1280,512]{2,1,0:T(8,128)(2,1)} %get-tuple-element.114), kind=kOutput, calls=%fused_computation.12 | convolution fusion | flops 5369233408 | bytes 16777216 | tf_op jit(solution)/shard_map/dot_general | solution.py:1310
  587.6 16.4 %reduce-scatter.8.cloned.1.call-done = bf16[128,512]{1,0:T(8,128)(2,1)} async-done(((bf16[1024,512]{1,0:T(8,128)(2,1)}), bf16[128,512]{1,0:T(8,128)(2,1)}) %reduce-scatter.8.cloned.1.call-update) | async-done | bytes 131088 | tf_op jit(solution)/shard_map/reduce_scatter | solution.py:1315
  604.0 44.4 %reduce-scatter.20.cloned.1.call-done = bf16[64,2048]{1,0:T(8,128)(2,1)} async-done(((bf16[512,2048]{1,0:T(8,128)(2,1)}), bf16[64,2048]{1,0:T(8,128)(2,1)}) %reduce-scatter.20.cloned.1.call-update) | async-done | bytes 262160 | tf_op jit(solution)/shard_map/reduce_scatter | solution.py:1315
  648.4 44.7 %reduce-scatter.16.cloned.1.call-done = bf16[256,512]{1,0:T(8,128)(2,1)} async-done(((bf16[2048,512]{1,0:T(8,128)(2,1)}), bf16[256,512]{1,0:T(8,128)(2,1)}) %reduce-scatter.16.cloned.1.call-update) | async-done | bytes 262160 | tf_op jit(solution)/shard_map/reduce_scatter | solution.py:1315
  693.1 44.4 %reduce-scatter.12.cloned.1.call-done = bf16[64,2048]{1,0:T(8,128)(2,1)} async-done(((bf16[512,2048]{1,0:T(8,128)(2,1)}), bf16[64,2048]{1,0:T(8,128)(2,1)}) %reduce-scatter.12.cloned.1.call-update) | async-done | bytes 262160 | tf_op jit(solution)/shard_map/reduce_scatter | solution.py:1315
  737.5 55.1 %reduce-scatter.14.cloned.1.call-done = bf16[128,2048]{1,0:T(8,128)(2,1)} async-done(((bf16[1024,2048]{1,0:T(8,128)(2,1)}), bf16[128,2048]{1,0:T(8,128)(2,1)}) %reduce-scatter.14.cloned.1.call-update) | async-done | bytes 524304 | tf_op jit(solution)/shard_map/reduce_scatter | solution.py:1315
  796.3 118.9 %all-reduce.3.cloned.1.call-done = (bf16[64,3,3,512]{3,2,1,0:T(4,128)(2,1)}, bf16[64,3,3,512]{3,2,1,0:T(4,128)(2,1)}, bf16[128,512]{1,0:T(8,128)(2,1)}, bf16[64,...) async-done(((bf16[64,3,3,512]{3,2,1,0:T(4,128)(2,1)}, bf16[64,3,3,512]{3,2,1,0:T(4,128)(2,1)}, ...) | async-done | bytes 2621456 | tf_op jit(solution)/shard_map/psum | solution.py:1316
  (182 shorter events, 180.7 us)
Async XLA Ops:
  7.2 576.2 %reduce-scatter.18.cloned.1.call-start = ((), (), s32[]{:S(2)}) async-start(), calls=%async_computation.12 | async-start | bytes 5308416 | tf_op jit(solution)/shard_map/reduce_scatter | solution.py:1315
  11.8 28.4 %copy-start.8 = (s32[80]{0:T(128)S(1)}, s32[80]{0:T(128)}, u32[]{:S(2)}) copy-start(s32[80]{0:T(128)} %param.26) | copy-start | bytes 964
  29.2 68.4 %collective-permute-start.1 = (f32[5,1,512]{2,1,0:T(1,128)}, f32[5,1,512]{2,1,0:T(1,128)S(1)}, u32[]{:S(2)}, u32[]{:S(2)}) collective-permute-start(f32[5,1,512]{2,1,0:T(1,128)} %get-tuple-element.75.centre_in.centre_m.centre), channel_id=1, source_target_pairs={{0,1},{1,2},{2,3},{4,5},{5,6},{6,7},{8,9},{9,10},{10,11},{12,13},{... | collective-permute-start | bytes 30728 | tf_op jit(solution)/shard_map/ppermute | solution.py:890
  35.5 62.0 %collective-permute-start = (bf16[2,640,512]{2,1,0:T(8,128)(2,1)S(1)}, bf16[2,640,512]{2,1,0:T(8,128)(2,1)}, u32[]{:S(2)}, u32[]{:S(2)}) collective-permute-start(bf16[2,640,512]{2,1,0:T(8,128)(2,1)S(1)} %slice_bitcast_fusion), channel_id=1, source_target_pairs={{0,1},{1,2},{2,3},{4,5},{5,6},{6,7},{8,9},{9,10},{10,11},{12,13},{... | collective-permute-start | bytes 3932168 | tf_op jit(solution)/shard_map/ppermute | solution.py:890
  171.7 35.4 %collective-permute-start.5 = (f32[5,1,512]{2,1,0:T(1,128)}, f32[5,1,512]{2,1,0:T(1,128)S(1)}, u32[]{:S(2)}, u32[]{:S(2)}) collective-permute-start(f32[5,1,512]{2,1,0:T(1,128)} %get-tuple-element.90.centre_in.centre_m), channel_id=1, source_target_pairs={{1,0},{2,1},{3,2},{5,4},{6,5},{7,6},{9,8},{10,9},{11,10},{13,12},{... | collective-permute-start | bytes 30728 | tf_op jit(solution)/shard_map/ppermute | solution.py:894
  173.0 34.1 %collective-permute-start.4 = (f32[5,1,512]{2,1,0:T(1,128)}, f32[5,1,512]{2,1,0:T(1,128)S(1)}, u32[]{:S(2)}, u32[]{:S(2)}) collective-permute-start(f32[5,1,512]{2,1,0:T(1,128)} %get-tuple-element.90.centre_in.centre_m), channel_id=1, source_target_pairs={{0,1},{1,2},{2,3},{4,5},{5,6},{6,7},{8,9},{9,10},{10,11},{12,13},{... | collective-permute-start | bytes 30728 | tf_op jit(solution)/shard_map/ppermute | solution.py:890
  178.9 28.8 %collective-permute-start.2 = (bf16[640,512]{1,0:T(8,128)(2,1)S(1)}, bf16[640,512]{1,0:T(8,128)(2,1)S(1)}, u32[]{:S(2)}, u32[]{:S(2)}) collective-permute-start(bf16[640,512]{1,0:T(8,128)(2,1)S(1)} %get-tuple-element.184), channel_id=1, source_target_pairs={{0,1},{1,2},{2,3},{4,5},{5,6},{6,7},{8,9},{9,10},{10,11},{12,13},{... | collective-permute-start | bytes 1966088 | tf_op jit(solution)/shard_map/ppermute | solution.py:890
  182.1 25.6 %collective-permute-start.3 = (bf16[640,512]{1,0:T(8,128)(2,1)S(1)}, bf16[640,512]{1,0:T(8,128)(2,1)S(1)}, u32[]{:S(2)}, u32[]{:S(2)}) collective-permute-start(bf16[640,512]{1,0:T(8,128)(2,1)S(1)} %get-tuple-element.185), channel_id=1, source_target_pairs={{1,0},{2,1},{3,2},{5,4},{6,5},{7,6},{9,8},{10,9},{11,10},{13,12},{... | collective-permute-start | bytes 1966088 | tf_op jit(solution)/shard_map/ppermute | solution.py:894
  224.3 90.7 %collective-permute-start.11 = (f32[5,1,512]{2,1,0:T(1,128)}, f32[5,1,512]{2,1,0:T(1,128)S(1)}, u32[]{:S(2)}, u32[]{:S(2)}) collective-permute-start(f32[5,1,512]{2,1,0:T(1,128)} %get-tuple-element.93.centre_in.centre_m.centre), channel_id=1, source_target_pairs={{1,0},{2,1},{3,2},{5,4},{6,5},{7,6},{9,8},{10,9},{11,10},{13,12},{... | collective-permute-start | bytes 30728 | tf_op jit(solution)/shard_map/ppermute | solution.py:894
  225.6 113.8 %collective-permute-start.10 = (f32[5,1,512]{2,1,0:T(1,128)}, f32[5,1,512]{2,1,0:T(1,128)S(1)}, u32[]{:S(2)}, u32[]{:S(2)}) collective-permute-start(f32[5,1,512]{2,1,0:T(1,128)} %get-tuple-element.93.centre_in.centre_m.centre), channel_id=1, source_target_pairs={{0,1},{1,2},{2,3},{4,5},{5,6},{6,7},{8,9},{9,10},{10,11},{12,13},{... | collective-permute-start | bytes 30728 | tf_op jit(solution)/shard_map/ppermute | solution.py:890
  240.7 100.6 %collective-permute-start.8 = (bf16[640,512]{1,0:T(8,128)(2,1)S(1)}, bf16[640,512]{1,0:T(8,128)(2,1)S(1)}, u32[]{:S(2)}, u32[]{:S(2)}) collective-permute-start(bf16[640,512]{1,0:T(8,128)(2,1)S(1)} %get-tuple-element.180), channel_id=1, source_target_pairs={{0,1},{1,2},{2,3},{4,5},{5,6},{6,7},{8,9},{9,10},{10,11},{12,13},{... | collective-permute-start | bytes 1966088 | tf_op jit(solution)/shard_map/ppermute | solution.py:890
  243.3 99.3 %collective-permute-start.9 = (bf16[640,512]{1,0:T(8,128)(2,1)S(1)}, bf16[640,512]{1,0:T(8,128)(2,1)S(1)}, u32[]{:S(2)}, u32[]{:S(2)}) collective-permute-start(bf16[640,512]{1,0:T(8,128)(2,1)S(1)} %get-tuple-element.181), channel_id=1, source_target_pairs={{1,0},{2,1},{3,2},{5,4},{6,5},{7,6},{9,8},{10,9},{11,10},{13,12},{... | collective-permute-start | bytes 1966088 | tf_op jit(solution)/shard_map/ppermute | solution.py:894
  312.3 31.6 %collective-permute-start.6 = (bf16[640,512]{1,0:T(8,128)(2,1)}, bf16[640,512]{1,0:T(8,128)(2,1)S(1)}, u32[]{:S(2)}, u32[]{:S(2)}) collective-permute-start(bf16[640,512]{1,0:T(8,128)(2,1)} %get-tuple-element.182), channel_id=1, source_target_pairs={{0,1},{1,2},{2,3},{4,5},{5,6},{6,7},{8,9},{9,10},{10,11},{12,13},{... | collective-permute-start | bytes 1966088 | tf_op jit(solution)/shard_map/ppermute | solution.py:890
  315.0 28.9 %collective-permute-start.7 = (bf16[640,512]{1,0:T(8,128)(2,1)}, bf16[640,512]{1,0:T(8,128)(2,1)}, u32[]{:S(2)}, u32[]{:S(2)}) collective-permute-start(bf16[640,512]{1,0:T(8,128)(2,1)} %get-tuple-element.183), channel_id=1, source_target_pairs={{1,0},{2,1},{3,2},{5,4},{6,5},{7,6},{9,8},{10,9},{11,10},{13,12},{... | collective-permute-start | bytes 1966088 | tf_op jit(solution)/shard_map/ppermute | solution.py:894
  339.4 132.7 %collective-permute-start.14 = (f32[5,1,512]{2,1,0:T(1,128)S(1)}, f32[5,1,512]{2,1,0:T(1,128)S(1)}, u32[]{:S(2)}, u32[]{:S(2)}) collective-permute-start(f32[5,1,512]{2,1,0:T(1,128)S(1)} %copy-done.15), channel_id=1, source_target_pairs={{1,0},{2,1},{3,2},{5,4},{6,5},{7,6},{9,8},{10,9},{11,10},{13,12},{... | collective-permute-start | bytes 30728 | tf_op jit(solution)/shard_map/ppermute | solution.py:894
  341.3 130.8 %collective-permute-start.13 = (bf16[640,512]{1,0:T(8,128)(2,1)}, bf16[640,512]{1,0:T(8,128)(2,1)S(1)}, u32[]{:S(2)}, u32[]{:S(2)}) collective-permute-start(bf16[640,512]{1,0:T(8,128)(2,1)} %slice_bitcast_fusion.1), channel_id=1, source_target_pairs={{1,0},{2,1},{3,2},{5,4},{6,5},{7,6},{9,8},{10,9},{11,10},{13,12},{... | collective-permute-start | bytes 1966088 | tf_op jit(solution)/shard_map/ppermute | solution.py:894
  387.2 198.3 %reduce-scatter.10.cloned.1.call-start = ((), (), s32[]{:S(2)}) async-start(), calls=%async_computation.8 | async-start | bytes 5308416 | tf_op jit(solution)/shard_map/reduce_scatter | solution.py:1315
  447.0 25.1 %collective-permute-start.12 = (bf16[640,512]{1,0:T(8,128)(2,1)S(1)}, bf16[640,512]{1,0:T(8,128)(2,1)S(1)}, u32[]{:S(2)}, u32[]{:S(2)}) collective-permute-start(bf16[640,512]{1,0:T(8,128)(2,1)S(1)} %slice_bitcast_fusion.2), channel_id=1, source_target_pairs={{1,0},{2,1},{3,2},{5,4},{6,5},{7,6},{9,8},{10,9},{11,10},{13,12},{... | collective-permute-start | bytes 1966088 | tf_op jit(solution)/shard_map/ppermute | solution.py:894
  473.3 32.2 %slice-start = ((s8[5242880]{0:T(1024)(128)(4,1)}), s8[1048576]{0:T(1024)(128)(4,1)S(1)}, s32[]{:S(2)}) async-start(s8[5242880]{0:T(1024)(128)(4,1)} %bitcast.206), calls=%async_computation.15 | async-start | bytes 2097152
  513.3 90.7 %reduce-scatter.8.cloned.1.call-start = ((), (), s32[]{:S(2)}) async-start(), calls=%async_computation.7 | async-start | bytes 1179648 | tf_op jit(solution)/shard_map/reduce_scatter | solution.py:1315
  552.1 96.3 %reduce-scatter.20.cloned.1.call-start = ((), (), s32[]{:S(2)}) async-start(), calls=%async_computation.13 | async-start | bytes 2359296 | tf_op jit(solution)/shard_map/reduce_scatter | solution.py:1315
  559.2 133.9 %reduce-scatter.16.cloned.1.call-start = ((), (), s32[]{:S(2)}) async-start(), calls=%async_computation.11 | async-start | bytes 2359296 | tf_op jit(solution)/shard_map/reduce_scatter | solution.py:1315
  566.3 171.3 %reduce-scatter.12.cloned.1.call-start = ((), (), s32[]{:S(2)}) async-start(), calls=%async_computation.9 | async-start | bytes 2359296 | tf_op jit(solution)/shard_map/reduce_scatter | solution.py:1315
  573.0 219.6 %reduce-scatter.14.cloned.1.call-start = ((), (), s32[]{:S(2)}) async-start(), calls=%async_computation.10 | async-start | bytes 4718592 | tf_op jit(solution)/shard_map/reduce_scatter | solution.py:1315
  583.2 209.4 %copy-start.9 = (f32[2,512]{1,0:T(2,128)S(1)}, f32[2,512]{1,0:T(2,128)}, u32[]{:S(2)}) copy-start(f32[2,512]{1,0:T(2,128)} %shard_map.432.sums_in) | copy-start | bytes 12292
  583.2 210.0 %copy-start.3 = (f32[2,2048]{1,0:T(2,128)S(1)}, f32[2,2048]{1,0:T(2,128)}, u32[]{:S(2)}) copy-start(f32[2,2048]{1,0:T(2,128)} %shard_map.430.sums_in) | copy-start | bytes 49156
  583.2 210.6 %copy-start.5 = (f32[3,2048]{1,0:T(4,128)S(1)}, f32[3,2048]{1,0:T(4,128)}, u32[]{:S(2)}) copy-start(f32[3,2048]{1,0:T(4,128)} %shard_map.436.sums_in) | copy-start | bytes 73732
  583.2 211.3 %copy-start.6 = (f32[2,512]{1,0:T(2,128)S(1)}, f32[2,512]{1,0:T(2,128)}, u32[]{:S(2)}) copy-start(f32[2,512]{1,0:T(2,128)} %shard_map.434.sums_in) | copy-start | bytes 12292
  583.2 211.8 %copy-start.10 = (f32[2,512]{1,0:T(2,128)S(1)}, f32[2,512]{1,0:T(2,128)}, u32[]{:S(2)}) copy-start(f32[2,512]{1,0:T(2,128)} %shard_map.438.sums_in) | copy-start | bytes 12292
  583.3 212.4 %copy-start.11 = (f32[2,512]{1,0:T(2,128)S(1)}, f32[2,512]{1,0:T(2,128)}, u32[]{:S(2)}) copy-start(f32[2,512]{1,0:T(2,128)} %shard_map.440.sums_in) | copy-start | bytes 12292
  583.3 331.9 %all-reduce.3.cloned.1.call-start = ((), (), s32[]{:S(2)}) async-start(), calls=%async_computation.14 | async-start | bytes 6029312 | tf_op jit(solution)/shard_map/psum | solution.py:1316
  794.5 133.0 %copy-start.4 = (f32[1,2048]{1,0:T(1,128)}, f32[1,2048]{1,0:T(1,128)S(1)}, u32[]{:S(2)}) copy-start(f32[1,2048]{1,0:T(1,128)S(1)} %get-tuple-element.187) | copy-start | bytes 24580
  (15 other events, 137.9 us)
Sparse Core Ops, SparseCore 0:
  387.3 55.7 reduce-scatter.17
  513.4 50.7 reduce-scatter.9
  568.0 35.9 reduce-scatter.7
  607.1 41.2 reduce-scatter.19
  651.9 41.2 reduce-scatter.15
  696.3 41.2 reduce-scatter.11
  741.3 51.3 reduce-scatter.13
  796.1 119.0 all-reduce.2
where the time goes:
time: 945 us; the launch traced here: 935 us
  Pallas kernels  412 us (44%)
  waiting for transfers between devices  324 us (34%)
  matrix products  66.1 us (7%)
  local copies, waits for them, and re-layouts  62.8 us (7%)
  starting transfers between devices  38.3 us (4%)
  other arithmetic  16.4 us (2%)
  between operations  15.3 us (2%)
    pallas_call x14, Pallas kernels, stage(): pl.pallas_call(kernel, grid=(blocks,), in_specs=[spec_of(x.shape, kind, b...  229 us
    reduce_scatter x7, waiting for transfers between devices, reduced(): shard = lax.psum_scatter(grad, 'img', scatter_dimension=0, tiled=True)  205 us
    pallas_call x12, Pallas kernels, __call__(): pl.pallas_call(functools.partial(sync_kernel, self.rows_n, self.img_n, me...  183 us
    psum x1, waiting for transfers between devices, reduced(): return lax.psum(shard, 'rows').astype(F32)  119 us
    dot_general x10, matrix products, weight_term(): lax.dot_general(values, upstream, (((0,), (0,)), ((), ())), preferred_ele...  66.1 us
    ppermute x7, starting transfers between devices, to_next(): return lax.ppermute(x, 'rows', [(i, i + 1) for i in range(peers - 1)])  27.1 us
    unnamed x60, local copies, waits for them, and re-layouts  23.8 us
  transfers between devices with their start and end apart: 23, of which 6 were waited for; matrix products, arithmetic and copies ran while one was open for 13% of the time, Pallas kernels for 33%

commit v1 on v0

--- a/solution.py
+++ b/solution.py
@@ -16,6 +16,7 @@
 IMAGES = 16
 VMEM_BYTES = 56 * 1024 * 1024
 MESH = pl.DeviceIdType.MESH
+BY_ROWS, BY_PLANES, FIRST_PLANE, BY_BLOCK, PAIR_BLOCK, WHOLE = range(6)
 
 
 def dot(a, b):
@@ -190,7 +191,22 @@
     return pl.program_id(0) == 0
 
 
-def split_kernel(image_ref, perm_ref, mask_ref, weight_ref, planes_ref, dev_ref, centre_ref, stats_ref, acc):
+def open_kernel(
+    image_ref,
+    perm_ref,
+    mask_ref,
+    mask_out,
+    weight_ref,
+    weight_skip,
+    planes_ref,
+    dev_ref,
+    centre_ref,
+    dev_skip,
+    centre_skip,
+    stats_ref,
+    acc,
+    acc_skip,
+):
     planes, low, _ = planes_ref.shape
     group = perm_ref.shape[0]
     part = group // planes
@@ -205,20 +221,15 @@
             planes_ref[p, g * part : (g + 1) * part, :] = moved[p * part : (p + 1) * part]
     for p in range(planes):
         acc[p] = dot(planes_ref[p], weight_ref[...])
+    width = acc.shape[-1]
     tally(
         first_step(),
         [(acc.at[p], mask_ref.at[p], dev_ref.at[p]) for p in range(planes)],
         centre_ref,
-        stats_ref,
-    )
-
-
-def skip_kernel(plane_ref, mask_ref, weight_ref, before_ref, dev_ref, centre_ref, stats_ref, acc, mine):
-    acc[...] = dot(plane_ref[...], weight_ref[...])
-    tally(first_step(), [(acc, mask_ref, dev_ref)], centre_ref, mine)
-    start = before_ref.shape[1]
-    stats_ref[:, :start] = before_ref[...]
-    stats_ref[:, start:] = mine[...]
+        stats_ref.at[:, :width],
+    )
+    acc_skip[...] = dot(planes_ref[0], weight_skip[...])
+    tally(first_step(), [(acc_skip, mask_out, dev_skip)], centre_skip, stats_ref.at[:, width:])
 
 
 def mid1_kernel(
@@ -272,7 +283,7 @@
 
     def tap(t, u):
         k = (3 * t + u) * width
-        return weight[:, k : k + width]
+        return weight[k : k + width]
 
     total = dot(hidden[0], tap(1, 1))
     total += dot(hidden[1], tap(1, 2))
@@ -376,14 +387,12 @@
             )
             for t in range(3):
                 for u in range(3):
-                    store(taps.at[3 * t + u], rows, lanes, shifted(lines[t], u - 1))
+                    start = (3 * t + u) * width + lanes.start
+                    store(taps, rows, slice(start, start + LANES), shifted(lines[t], u - 1))
             return carry
 
         sweep(low, step, 0)
-    total = dot(taps[0], weight[:, :width])
-    for k in range(1, 9):
-        total += dot(taps[k], weight[:, k * width : (k + 1) * width])
-    acc[...] = total
+    acc[...] = dot(taps[...], weight[...])
     tally(first_step(), [(acc, mask, dev_out)], centre_out, stats_out)
 
 
@@ -525,7 +534,10 @@
             return carry
 
         sweep(low, step, 0)
-    acc[...] = dot_t(views[...], weight[...])
+    total = dot_t(views[:, :width], weight[:width])
+    for k in range(width, 9 * width, width):
+        total += dot_t(views[:, k : k + width], weight[k : k + width])
+    acc[...] = total
     gate_sums(first_step(), acc, dev_m, centre_m, stats_m, gain_m, shift_m, mask, gn_m, sums_m, 0)
 
 
@@ -614,8 +626,8 @@
     ga_a,
     ga_b,
     gn_m,
+    grad_skip,
     sums_m,
-    grad_skip,
     acc,
 ):
     for lanes in lane_blocks(dev_a.shape[1]):
@@ -690,7 +702,7 @@
 
     def tap(t, u):
         k = (3 * t + u) * width
-        return weight[:, k : k + width]
+        return weight[k : k + width]
 
     acc[0] = dot_t(view(1), tap(1, 1))
     acc[1] = dot_t(view(1), tap(1, 2)) + dot_t(view(2), tap(1, 0))
@@ -742,39 +754,44 @@
 
 
 def spec_of(shape, kind, blocks):
-    if kind == "rows":
+    if kind == BY_ROWS:
         return pl.BlockSpec((shape[0] // blocks, shape[1]), lambda b: (b, 0))
-    if kind == "planes":
+    if kind == BY_PLANES:
         return pl.BlockSpec((shape[0], shape[1] // blocks, shape[2]), lambda b: (0, b, 0))
-    if kind == "plane0":
+    if kind == FIRST_PLANE:
         return pl.BlockSpec((None, shape[1] // blocks, shape[2]), lambda b: (0, b, 0))
-    if kind == "each":
+    if kind == BY_BLOCK:
         return pl.BlockSpec((None,) + tuple(shape[1:]), lambda b: (b, 0, 0))
-    if kind == "each2":
+    if kind == PAIR_BLOCK:
         return pl.BlockSpec((2, None) + tuple(shape[2:]), lambda b: (0, b, 0, 0))
     zero = (0,) * len(shape)
     return pl.BlockSpec(tuple(shape), lambda b: zero, pipeline_mode=pl.Buffered(1))
 
 
 def out_spec(shape, kind, blocks):
-    if kind == "all":
+    if kind == WHOLE:
         zero = (0,) * len(shape)
         return pl.BlockSpec(tuple(shape), lambda b: zero)
     return spec_of(shape, kind, blocks)
 
 
 def stage(kernel, blocks, ins, outs, scratch=(), flops=0):
+    return call(kernel, blocks, ins, outs, scratch, flops, [], [], {})
+
+
+def call(kernel, blocks, ins, outs, scratch, flops, more_specs, more_shapes, params):
     moved = sum(x.size * x.dtype.itemsize for x, _ in ins)
     moved += sum(int(np.prod(s)) * jnp.dtype(d).itemsize for s, d, _ in outs)
+    made = [pltpu.VMEM(*item) if isinstance(item, tuple) else item for item in scratch]
     return pl.pallas_call(
         kernel,
         grid=(blocks,),
         in_specs=[spec_of(x.shape, kind, blocks) for x, kind in ins],
-        out_specs=[out_spec(s, kind, blocks) for s, _, kind in outs],
-        out_shape=[jax.ShapeDtypeStruct(s, d) for s, d, _ in outs],
-        scratch_shapes=[pltpu.VMEM(s, d) for s, d in scratch],
+        out_specs=[out_spec(s, kind, blocks) for s, _, kind in outs] + more_specs,
+        out_shape=[jax.ShapeDtypeStruct(s, d) for s, d, _ in outs] + more_shapes,
+        scratch_shapes=made,
         compiler_params=pltpu.CompilerParams(
-            dimension_semantics=("arbitrary",), vmem_limit_bytes=VMEM_BYTES
+            dimension_semantics=("arbitrary",), vmem_limit_bytes=VMEM_BYTES, **params
         ),
         cost_estimate=pl.CostEstimate(flops=flops, bytes_accessed=moved, transcendentals=0),
     )(*[x for x, _ in ins])
@@ -802,96 +819,621 @@
     return jnp.concatenate([count, mean, squares], axis=0)
 
 
-def sync_kernel(rows_n, img_n, merge, widths, mine, *refs):
-    outs = refs[: len(widths)]
-    buf_r, buf_i, part, send_r, recv_r, send_i, recv_i = refs[len(widths) :]
-    row, img = lax.axis_index("rows"), lax.axis_index("img")
-    barrier = pltpu.get_barrier_semaphore()
-    for k in range(1, rows_n):
-        peer = lax.rem(row + k, rows_n)
-        pl.semaphore_signal(barrier, inc=1, device_id={"rows": peer}, device_id_type=MESH)
-    for k in range(1, img_n):
-        peer = lax.rem(img + k, img_n)
-        pl.semaphore_signal(barrier, inc=1, device_id={"img": peer}, device_id_type=MESH)
-    pl.semaphore_wait(barrier, rows_n + img_n - 2)
-    copies = []
-
-    def exchange(axis, me, peers, source, buf, send, recv):
-        for k in range(1, peers):
-            copy = pltpu.make_async_remote_copy(
+class Exchange:
+    def __init__(self, rows_n, img_n, blocks):
+        self.rows_n, self.img_n, self.blocks = rows_n, img_n, blocks
+        self.calls = 0
+
+    def __call__(
+        self, kernel, ins, outs, merge, lines, widths, scratch=(), flops=0, edges=(), centres=None, edge=0
+    ):
+        ident, self.calls = self.calls, self.calls + 1
+        total, dma = sum(widths), pltpu.SemaphoreType.DMA
+        any_space = pl.BlockSpec(memory_space=pl.ANY)
+        specs = [out_spec((lines, w), WHOLE, 1) for w in widths]
+        shapes = [jax.ShapeDtypeStruct((lines, w), F32) for w in widths]
+        extra = []
+        if edges:
+            middle = outs[edges[0][0]][0][-1]
+            specs.append(any_space)
+            shapes.append(jax.ShapeDtypeStruct((len(edges), edge, middle), BF16))
+            extra += [
+                ((len(edges), edge, middle), BF16),
+                dma((len(edges), self.blocks)),
+                dma((len(edges), self.blocks)),
+                dma((len(edges),)),
+            ]
+        if centres:
+            count, shape = len(centres[1]), outs[centres[0]][0]
+            specs.append(any_space)
+            shapes.append(jax.ShapeDtypeStruct((count,) + tuple(shape), F32))
+            extra += [(tuple(shape), F32), dma((count,)), dma((count,)), dma((count,))]
+        extra += [
+            ((self.rows_n, lines, total), F32),
+            ((self.img_n, lines, total), F32),
+            ((lines, total), F32),
+            dma((self.rows_n,)),
+            dma((self.rows_n,)),
+            dma((self.img_n,)),
+            dma((self.img_n,)),
+        ]
+        return call(
+            functools.partial(
+                self.kernel, kernel, len(ins), len(outs), len(scratch), merge, widths, edges, centres
+            ),
+            self.blocks,
+            ins,
+            outs,
+            [((lines, total), F32)] + list(scratch) + extra,
+            flops,
+            specs,
+            shapes,
+            dict(collective_id=ident, has_side_effects=True),
+        )
+
+    def kernel(self, kernel, ins_n, outs_n, scratch_n, merge, widths, edges, centres, *refs):
+        rows_n, img_n, blocks = self.rows_n, self.img_n, self.blocks
+        refs = list(refs)
+
+        def take(count):
+            taken = refs[:count]
+            del refs[:count]
+            return taken
+
+        ins, outs, totals = take(ins_n), take(outs_n), take(len(widths))
+        halo = take(1)[0] if edges else None
+        halo_centres = take(1)[0] if centres else None
+        mine = take(1)[0]
+        scratch = take(scratch_n)
+        if edges:
+            edge_buf, edge_send, edge_recv, edge_local = take(4)
+        if centres:
+            centre_buf, centre_send, centre_recv, centre_local = take(4)
+        buf_r, buf_i, part, send_r, recv_r, send_i, recv_i = refs
+        block = pl.program_id(0)
+        row, img = lax.axis_index("rows"), lax.axis_index("img")
+        barrier = pltpu.get_barrier_semaphore()
+
+        @pl.when(block == 0)
+        def _():
+            for k in range(1, rows_n):
+                peer = {"rows": lax.rem(row + k, rows_n)}
+                pl.semaphore_signal(barrier, inc=1, device_id=peer, device_id_type=MESH)
+            for k in range(1, img_n):
+                peer = {"img": lax.rem(img + k, img_n)}
+                pl.semaphore_signal(barrier, inc=1, device_id=peer, device_id_type=MESH)
+
+        kernel(*ins, *outs, mine, *scratch)
+
+        @pl.when(block == 0)
+        def _():
+            pl.semaphore_wait(barrier, rows_n + img_n - 2)
+
+        def remote(source, target, send, recv, peer):
+            return pltpu.make_async_remote_copy(
                 src_ref=source,
-                dst_ref=buf.at[me],
-                send_sem=send.at[k],
-                recv_sem=recv.at[me],
-                device_id={axis: lax.rem(me + k, peers)},
+                dst_ref=target,
+                send_sem=send,
+                recv_sem=recv,
+                device_id=peer,
                 device_id_type=MESH,
             )
-            copy.start()
-            copies.append(copy)
-        buf[pl.ds(me, 1)] = source[...][None]
-        for k in range(1, peers):
-            peer = lax.rem(me + k, peers)
-            pltpu.make_async_remote_copy(
-                src_ref=source,
-                dst_ref=buf.at[peer],
-                send_sem=send.at[k],
-                recv_sem=recv.at[peer],
-                device_id={axis: peer},
-                device_id_type=MESH,
-            ).wait_recv()
-
-    exchange("rows", row, rows_n, mine, buf_r, send_r, recv_r)
-    part[...] = merge_rows(buf_r, rows_n, merge, False)
-    exchange("img", img, img_n, part, buf_i, send_i, recv_i)
-    total = merge_rows(buf_i, img_n, merge, True)
-    start = 0
-    for out, width in zip(outs, widths):
-        out[...] = total[:, start : start + width]
-        start += width
-    for copy in copies:
-        copy.wait_send()
-
-
-class Sync:
-    def __init__(self, rows_n, img_n):
-        self.rows_n, self.img_n = rows_n, img_n
-        self.ids = {}
-
-    def __call__(self, mine, merge, widths=None):
-        lines, width = mine.shape
-        widths = widths or (width,)
-        key = (merge, lines, tuple(widths))
-        ident = self.ids.setdefault(key, len(self.ids))
-        shape = (lines, width)
-        dma = pltpu.SemaphoreType.DMA
-        out = pl.pallas_call(
-            functools.partial(sync_kernel, self.rows_n, self.img_n, merge, widths),
-            in_specs=[pl.BlockSpec(memory_space=pltpu.VMEM)],
-            out_specs=[pl.BlockSpec(memory_space=pltpu.VMEM)] * len(widths),
-            out_shape=[jax.ShapeDtypeStruct((lines, w), F32) for w in widths],
-            scratch_shapes=[
-                pltpu.VMEM((self.rows_n,) + shape, F32),
-                pltpu.VMEM((self.img_n,) + shape, F32),
-                pltpu.VMEM(shape, F32),
-                dma((self.rows_n,)),
-                dma((self.rows_n,)),
-                dma((self.img_n,)),
-                dma((self.img_n,)),
-            ],
-            compiler_params=pltpu.CompilerParams(collective_id=ident, has_side_effects=True),
-            cost_estimate=pl.CostEstimate(
-                flops=12_000_000_000, bytes_accessed=1_000_000, transcendentals=0
+
+        def sends(direction):
+            return row < rows_n - 1 if direction > 0 else row > 0
+
+        def receives(direction):
+            return row > 0 if direction > 0 else row < rows_n - 1
+
+        if edges:
+            some = edge_buf.shape[1] // blocks
+
+            def edge_copy(e, b):
+                here = pl.ds(pl.multiple_of(b * some, some), some)
+                return remote(
+                    edge_buf.at[e, here],
+                    halo.at[e, here],
+                    edge_send.at[e, b],
+                    edge_recv.at[e, b],
+                    {"rows": row + edges[e][3]},
+                )
+
+            for e, (out, plane, last_row, direction) in enumerate(edges):
+                source = outs[out] if plane is None else outs[out].at[plane]
+                here = pl.ds(pl.multiple_of(block * some, some), some)
+                for lanes in lane_blocks(source.shape[1]):
+                    value = load(source, slice(None), lanes)
+                    lines = value.reshape((some // 8, -1) + value.shape[1:])
+                    store(edge_buf.at[e], here, lanes, lines[:, -1 if last_row else 0])
+
+                @pl.when(sends(direction))
+                def _(e=e):
+                    edge_copy(e, block).start()
+
+        if centres:
+            centre_buf[pl.ds(block, 1)] = outs[centres[0]][...][None]
+
+        def exchange(axis, me, peers, source, buf, send, recv):
+            copies = []
+            for k in range(1, peers):
+                peer = {axis: lax.rem(me + k, peers)}
+                copies.append(remote(source, buf.at[me], send.at[k], recv.at[me], peer))
+                copies[-1].start()
+            buf[pl.ds(me, 1)] = source[...][None]
+            for k in range(1, peers):
+                peer = lax.rem(me + k, peers)
+                remote(source, buf.at[peer], send.at[k], recv.at[peer], {axis: peer}).wait_recv()
+            return copies
+
+        @pl.when(block == blocks - 1)
+        def _():
+            def centre_copy(k):
+                peer = {"rows": row + centres[1][k]}
+                return remote(
+                    centre_buf, halo_centres.at[k], centre_send.at[k], centre_recv.at[k], peer
+                )
+
+            directions = centres[1] if centres else ()
+            for k, direction in enumerate(directions):
+
+                @pl.when(sends(direction))
+                def _(k=k):
+                    centre_copy(k).start()
+
+            copies = exchange("rows", row, rows_n, mine, buf_r, send_r, recv_r)
+            part[...] = merge_rows(buf_r, rows_n, merge, False)
+            copies += exchange("img", img, img_n, part, buf_i, send_i, recv_i)
+            total = merge_rows(buf_i, img_n, merge, True)
+            start = 0
+            for out, width in zip(totals, widths):
+                out[...] = total[:, start : start + width]
+                start += width
+            for k, direction in enumerate(directions):
+                own = pltpu.make_async_copy(centre_buf, halo_centres.at[k], centre_local.at[k])
+
+                @pl.when(receives(direction))
+                def _(k=k):
+                    centre_copy(k).wait_recv()
+
+                @pl.when(jnp.logical_not(receives(direction)))
+                def _(own=own):
+                    own.start()
+                    own.wait()
+
+                @pl.when(sends(direction))
+                def _(k=k):
+                    centre_copy(k).wait_send()
+
+            for e, spec in enumerate(edges):
+                own = pltpu.make_async_copy(edge_buf.at[e], halo.at[e], edge_local.at[e])
+
+                @pl.when(receives(spec[3]))
+                def _(e=e):
+                    for b in range(blocks):
+                        edge_copy(e, b).wait_recv()
+
+                @pl.when(jnp.logical_not(receives(spec[3])))
+                def _(own=own):
+                    own.start()
+                    own.wait()
+
+                @pl.when(sends(spec[3]))
+                def _(e=e):
+                    for b in range(blocks):
+                        edge_copy(e, b).wait_send()
+
+            for copy in copies:
+                copy.wait_send()
+
+
+CHUNK_ROWS = 64
+CHUNK_LANES = 1024
+
+
+HID_MID2, GA_OUT2, HID_IN2, VIEWS2, FIRST, GA_IN2, HID_MID1, GA_OUT1, GA_SKIP, VIEWS1 = range(10)
+HID, PLANE, GA_IN1 = 10, 14, 18
+ONE, TWO, HALF, QUAD, DEEP = range(5)
+WIDTHS = {ONE: (512, 1024), TWO: (1024, 512), HALF: (512, 512), QUAD: (1024, 256), DEEP: (1024, 512)}
+
+
+def plan_jobs():
+    chunks = [[(ONE, 0, HID_MID2, 0, GA_OUT2, 1024 * k)] for k in range(2)]
+    chunks += [[(ONE, 0, HID_IN2, 0, VIEWS2, 1024 * k)] for k in range(4)]
+    chunks += [[(HALF, 0, HID_IN2, 0, VIEWS2, 4096), (HALF, 1, HID, 0, VIEWS1, 512)]]
+    chunks += [[(QUAD, h, FIRST, 1024 * h, GA_IN2, 256 * k) for h in range(2)] for k in range(2)]
+    chunks += [[(DEEP, p, PLANE + p, 0, GA_IN1 + p, 0) for p in range(4)]]
+    chunks += [[(ONE, 0, HID_MID1, 0, GA_OUT1, 1024 * k)] for k in range(2)]
+    chunks += [[(TWO, 0, PLANE, 0, GA_SKIP, 512 * k)] for k in range(4)]
+    chunks += [[(ONE, 0, HID + 1, 0, VIEWS1, 512)], [(ONE, 0, HID + 2, 0, VIEWS1, 0)]]
+    chunks += [[(ONE, 0, HID + 3, 0, VIEWS1, 1024 * k)] for k in range(2)]
+    return chunks
+
+
+def weights_kernel(
+    rows_n,
+    hid_mid2,
+    ga_out2,
+    hid_in2,
+    views2,
+    first_low,
+    ga_in2,
+    hid_mid1,
+    ga_out1,
+    planes,
+    ga_skip,
+    hid_in1,
+    views1,
+    ga_in1,
+    done,
+    lhs_buf,
+    rhs_buf,
+    deep,
+    chunk_buf,
+    own,
+    got1,
+    got2a,
+    got2b,
+    got3a,
+    got3b,
+    got_low,
+    got_high,
+    lhs_sem,
+    rhs_sem,
+    *sems,
+):
+    (s1, r1, s2a, r2a, s2b, r2b, s3a, r3a, s3b, r3b, s_up, r_low, s_down, r_high, b_up, b_down, r_back) = sems
+    sources = [hid_mid2, ga_out2, hid_in2, views2, first_low, ga_in2, hid_mid1, ga_out1, ga_skip, views1]
+    for stack in (hid_in1, planes, ga_in1):
+        sources += [stack.at[p] for p in range(4)]
+    chunks = plan_jobs()
+    jobs = [job for chunk in chunks for job in chunk]
+    count = len(chunks)
+    depth = chunk_buf.shape[0]
+    img, z = lax.axis_index("img"), lax.axis_index("rows")
+    y, x, c = img // 4, lax.rem(img // 2, 2), lax.rem(img, 2)
+    root = rows_n // 2
+    sibling = {"img": img + 1 - 2 * c}
+    beside_x = {"img": img + 2 - 4 * x}
+    beside_y = {"img": img + 4 - 8 * y}
+    higher, lower = {"rows": z + 1}, {"rows": z - 1}
+    half = CHUNK_LANES // 2
+    left, right = slice(0, half), slice(half, 2 * half)
+
+    def fetch(index):
+        kind, _, lhs, lhs_start, rhs, rhs_start = jobs[index]
+        lhs_width, rhs_width = WIDTHS[kind]
+        slot = index % 2
+        return (
+            pltpu.make_async_copy(
+                sources[lhs].at[:, lhs_start : lhs_start + lhs_width],
+                lhs_buf.at[slot, :, :lhs_width],
+                lhs_sem.at[slot],
             ),
-        )(mine)
-        return out[0] if len(widths) == 1 else out
-
-
-def to_next(x, peers):
-    return lax.ppermute(x, "rows", [(i, i + 1) for i in range(peers - 1)])
-
-
-def to_previous(x, peers):
-    return lax.ppermute(x, "rows", [(i + 1, i) for i in range(peers - 1)])
+            pltpu.make_async_copy(
+                sources[rhs].at[:, rhs_start : rhs_start + rhs_width],
+                rhs_buf.at[slot, :, :rhs_width],
+                rhs_sem.at[slot],
+            ),
+        )
+
+    for copy in fetch(0):
+        copy.start()
+
+    barrier = pltpu.get_barrier_semaphore()
+    for peer in (sibling, beside_x, beside_y):
+        pl.semaphore_signal(barrier, inc=1, device_id=peer, device_id_type=MESH)
+
+    @pl.when(z > 0)
+    def _():
+        pl.semaphore_signal(barrier, inc=1, device_id=lower, device_id_type=MESH)
+
+    @pl.when(z < rows_n - 1)
+    def _():
+        pl.semaphore_signal(barrier, inc=1, device_id=higher, device_id_type=MESH)
+
+    pl.semaphore_wait(barrier, 3 + jnp.minimum(z, 1) + jnp.minimum(rows_n - 1 - z, 1))
+
+    def put(slot, result, first, parts):
+        width = CHUNK_LANES // parts
+        rows = CHUNK_ROWS
+        for m in range(result.shape[0] // (rows * parts)):
+            shard = first + m
+            for h in range(parts):
+                piece = result[(m * parts + h) * rows : (m * parts + h + 1) * rows]
+                chunk_buf[slot, shard // 4, shard // 2 % 2, shard % 2, :, h * width : (h + 1) * width] = piece
+
+    def multiply(index, slot):
+        kind, part = jobs[index][:2]
+        lhs_width, rhs_width = WIDTHS[kind]
+        here = index % 2
+
+        def product():
+            return lax.dot_general(
+                lhs_buf[here, :, :lhs_width],
+                rhs_buf[here, :, :rhs_width],
+                (((0,), (0,)), ((), ())),
+                preferred_element_type=F32,
+            )
+
+        if kind == ONE:
+            put(slot, product().astype(BF16), 0, 1)
+        elif kind == TWO:
+            put(slot, product().astype(BF16), 0, 2)
+        elif kind == QUAD:
+            put(slot, product().astype(BF16), 4 * part, 4)
+        elif kind == HALF:
+            result = product().astype(BF16)
+            for m in range(8):
+                piece = result[m * CHUNK_ROWS : (m + 1) * CHUNK_ROWS]
+                chunk_buf[slot, m // 4, m // 2 % 2, m % 2, :, (left, right)[part]] = piece
+        elif part == 0:
+            deep[...] = product()
+        elif part == 3:
+            put(slot, (deep[...] + product()).astype(BF16), 0, 2)
+        else:
+            deep[...] += product()
+
+    def remote(source, target, send, recv, peer):
+        return pltpu.make_async_remote_copy(
+            src_ref=source,
+            dst_ref=target,
+            send_sem=send,
+            recv_sem=recv,
+            device_id=peer,
+            device_id_type=MESH,
+        )
+
+    def to_core(t):
+        source = chunk_buf.at[lax.rem(t, depth), :, :, 1 - c]
+        return remote(source, got1.at[t], s1.at[t], r1.at[t], sibling)
+
+    def to_2a(t):
+        return remote(own.at[t, :, 1 - x, :, left], got2a.at[t], s2a.at[t], r2a.at[t], beside_x)
+
+    def to_2b(t):
+        return remote(own.at[t, 1 - y, :, :, right], got2b.at[t], s2b.at[t], r2b.at[t], beside_y)
+
+    def to_3a(t):
+        return remote(own.at[t, 1 - y, x, :, left], got3a.at[t], s3a.at[t], r3a.at[t], beside_y)
+
+    def to_3b(t):
+        return remote(own.at[t, y, 1 - x, :, right], got3b.at[t], s3b.at[t], r3b.at[t], beside_x)
+
+    def up(t):
+        return remote(own.at[t, y, x], got_low.at[t], s_up.at[t], r_low.at[t], higher)
+
+    def down(t):
+        return remote(own.at[t, y, x], got_high.at[t], s_down.at[t], r_high.at[t], lower)
+
+    def back_up(t):
+        return remote(done.at[t], done.at[t], b_up.at[t], r_back.at[t], higher)
+
+    def back_down(t):
+        return remote(done.at[t], done.at[t], b_down.at[t], r_back.at[t], lower)
+
+    def compute(t):
+        @pl.when(t >= depth)
+        def _():
+            to_core(t - depth).wait_send()
+
+        slot = lax.rem(t, depth)
+        index = 0
+        for k, chunk in enumerate(chunks):
+            first = index
+            index += len(chunk)
+
+            @pl.when(t == k)
+            def _(first=first, chunk=chunk):
+                for n in range(first, first + len(chunk)):
+                    for copy in fetch(n):
+                        copy.wait()
+                    if n + 1 < len(jobs):
+                        for copy in fetch(n + 1):
+                            copy.start()
+                    multiply(n, slot)
+
+        to_core(t).start()
+
+    def stage1(t):
+        to_core(t).wait_recv()
+        slot = lax.rem(t, depth)
+        for a in range(2):
+            for b in range(2):
+                own[t, a, b] = chunk_buf[slot, a, b, c] + got1[t, a, b]
+        to_2a(t).start()
+        to_2b(t).start()
+
+    def stage2(t):
+        to_2a(t).wait_recv()
+        for a in range(2):
+            own[t, a, x, :, left] = own[t, a, x, :, left] + got2a[t, a]
+        to_3a(t).start()
+        to_2b(t).wait_recv()
+        for a in range(2):
+            own[t, y, a, :, right] = own[t, y, a, :, right] + got2b[t, a]
+        to_3b(t).start()
+
+    def stage3(t):
+        to_3a(t).wait_recv()
+        own[t, y, x, :, left] = own[t, y, x, :, left] + got3a[t]
+        to_3b(t).wait_recv()
+        own[t, y, x, :, right] = own[t, y, x, :, right] + got3b[t]
+
+        @pl.when(z == 0)
+        def _():
+            up(t).start()
+
+        @pl.when(z == rows_n - 1)
+        def _():
+            down(t).start()
+
+    def stage4(t):
+        @pl.when((z > 0) & (z < root))
+        def _():
+            up(t).wait_recv()
+            own[t, y, x] = own[t, y, x] + got_low[t]
+            up(t).start()
+
+        @pl.when((z < rows_n - 1) & (z > root))
+        def _():
+            down(t).wait_recv()
+            own[t, y, x] = own[t, y, x] + got_high[t]
+            down(t).start()
+
+    def stage5(t):
+        @pl.when(z == root)
+        def _():
+            up(t).wait_recv()
+            down(t).wait_recv()
+            total = own[t, y, x].astype(F32) + got_low[t].astype(F32) + got_high[t].astype(F32)
+            done[t] = total.astype(BF16)
+            back_up(t).start()
+            back_down(t).start()
+
+    def stage6(t):
+        @pl.when(z > root)
+        def _():
+            back_up(t).wait_recv()
+
+            @pl.when(z < rows_n - 1)
+            def _():
+                back_up(t).start()
+
+        @pl.when((z < root) & (z > 0))
+        def _():
+            back_down(t).wait_recv()
+            back_down(t).start()
+
+    def stage7(t):
+        @pl.when(z == 0)
+        def _():
+            back_down(t).wait_recv()
+
+    stages = (compute, stage1, stage2, stage3, stage4, stage5, stage6, stage7)
+
+    def step(s, carry):
+        for lag, work in enumerate(stages):
+            t = s - lag
+
+            @pl.when((t >= 0) & (t < count))
+            def _(t=t, work=work):
+                work(t)
+
+        return carry
+
+    lax.fori_loop(0, count + len(stages) - 1, step, 0)
+
+    def finish(t, carry):
+        @pl.when(t >= count - depth)
+        def _():
+            to_core(t).wait_send()
+
+        for copy in (to_2a(t), to_2b(t), to_3a(t), to_3b(t)):
+            copy.wait_send()
+
+        @pl.when(z < root)
+        def _():
+            up(t).wait_send()
+
+        @pl.when(z > root)
+        def _():
+            down(t).wait_send()
+
+        @pl.when((z >= root) & (z < rows_n - 1))
+        def _():
+            back_up(t).wait_send()
+
+        @pl.when((z <= root) & (z > 0))
+        def _():
+            back_down(t).wait_send()
+
+        return carry
+
+    lax.fori_loop(0, count, finish, 0)
+
+
+def summed_weights(rows_n, ident, operands):
+    count = len(plan_jobs())
+    low = operands[0].shape[0]
+    rows, lanes = CHUNK_ROWS, CHUNK_LANES
+    dma = pltpu.SemaphoreType.DMA
+    depth = 3
+    buffers = [
+        (2, low, 1024),
+        (2, low, 1024),
+        None,
+        (depth, 2, 2, 2, rows, lanes),
+        (count, 2, 2, rows, lanes),
+        (count, 2, 2, rows, lanes),
+        (count, 2, rows, lanes // 2),
+        (count, 2, rows, lanes // 2),
+        (count, rows, lanes // 2),
+        (count, rows, lanes // 2),
+        (count, rows, lanes),
+        (count, rows, lanes),
+    ]
+    scratch = [pltpu.VMEM(b, BF16) if b else pltpu.VMEM((1024, 512), F32) for b in buffers]
+    return pl.pallas_call(
+        functools.partial(weights_kernel, rows_n),
+        in_specs=[pl.BlockSpec(memory_space=pl.ANY)] * len(operands),
+        out_specs=pl.BlockSpec(memory_space=pltpu.VMEM),
+        out_shape=jax.ShapeDtypeStruct((count, rows, lanes), BF16),
+        scratch_shapes=scratch + [dma((2,)), dma((2,))] + [dma((count,))] * 17,
+        compiler_params=pltpu.CompilerParams(
+            collective_id=ident, has_side_effects=True, vmem_limit_bytes=63 * 1024 * 1024
+        ),
+        cost_estimate=pl.CostEstimate(
+            flops=40_000_000_000, bytes_accessed=100_000_000, transcendentals=0
+        ),
+    )(*operands)
+
+
+def unpack_kernel(sums_n, done, *refs):
+    sums, outs = refs[:sums_n], refs[sums_n:]
+    in1, mid1, out1, skip, in2, mid2, out2 = outs[:7]
+    rows, lanes = CHUNK_ROWS, CHUNK_LANES
+    half = lanes // 2
+
+    def wide(k):
+        return done[k].astype(F32)
+
+    def stacked(first, count, parts, out):
+        width = lanes // parts
+        for k in range(count):
+            for h in range(parts):
+                piece = done[first + k, :, h * width : (h + 1) * width]
+                out[h * rows : (h + 1) * rows, k * width : (k + 1) * width] = piece.astype(F32)
+
+    for k in range(2):
+        out2[:, k * lanes : (k + 1) * lanes] = wide(k)
+        out1[:, k * lanes : (k + 1) * lanes] = wide(10 + k)
+    taps2 = [(2 + k // 2, k % 2) for k in range(8)] + [(6, 0)]
+    taps1 = [(19, 1), (17, 0), (18, 0), (16, 1), (6, 1), (16, 0), (19, 0), (17, 1), (18, 1)]
+    for out, taps in ((mid1, taps1), (mid2, taps2)):
+        for k, (chunk, side) in enumerate(taps):
+            out[k] = done[chunk, :, side * half : (side + 1) * half].astype(F32)
+    stacked(7, 2, 4, in2)
+    stacked(9, 1, 2, in1)
+    stacked(12, 4, 2, skip)
+    rest = list(outs[7:])
+    for ref in sums:
+        for k in range(ref.shape[0]):
+            rest.pop(0)[...] = ref[k : k + 1, :]
+
+
+def unpack(done, sums):
+    rows = CHUNK_ROWS
+    shapes = [(128, 512), (9, rows, 512), (rows, 2048), (128, 2048), (256, 512), (9, rows, 512), (rows, 2048)]
+    shapes += [(1, x.shape[1]) for x in sums for _ in range(x.shape[0])]
+    vmem = pl.BlockSpec(memory_space=pltpu.VMEM)
+    outs = pl.pallas_call(
+        functools.partial(unpack_kernel, len(sums)),
+        in_specs=[vmem] * (1 + len(sums)),
+        out_specs=[vmem] * len(shapes),
+        out_shape=[jax.ShapeDtypeStruct(shape, F32) for shape in shapes],
+        compiler_params=pltpu.CompilerParams(vmem_limit_bytes=32 * 1024 * 1024),
+    )(done, *sums)
+    return outs[:7], [x.reshape(-1) for x in outs[7:]]
 
 
 def lanes128(mask):
@@ -932,8 +1474,7 @@
     blocks = images // IMAGES
     per_block = low // blocks
     edge = images * cols_low
-    sync = Sync(rows_n, img_n)
-    run = functools.partial(stage, blocks=blocks)
+    run = Exchange(rows_n, img_n, blocks)
 
     row0 = lax.axis_index("rows") * rows_here
     half = extent // 2
@@ -978,372 +1519,365 @@
     g_out1, s_out1, g_skip, s_skip = row(gain_out1), row(shift_out1), row(gain_skip), row(shift_skip)
     g_in2, s_in2, g_mid2, s_mid2 = row(gain_in2), row(shift_in2), row(gain_mid2), row(shift_mid2)
     g_out2, s_out2 = row(gain_out2), row(shift_out2)
-    kernel_mid1 = weight_mid1.reshape(middle, 9 * middle)
-    kernel_mid2 = weight_mid2.reshape(middle, 9 * middle)
+    kernel_mid1 = weight_mid1.transpose(1, 2, 0, 3).reshape(9 * middle, middle)
+    kernel_mid2 = weight_mid2.transpose(1, 2, 0, 3).reshape(9 * middle, middle)
     cot = cotangent.reshape(low, outputs)
 
-    dev_mid_out = [
-        ((low, middle), BF16, "rows"),
-        ((blocks, 1, middle), F32, "each"),
-        ((3, middle), F32, "all"),
-    ]
-    dev_out_out = [
-        ((low, outputs), BF16, "rows"),
-        ((blocks, 1, outputs), F32, "each"),
-        ((3, outputs), F32, "all"),
-    ]
+    dev_mid_out = [((low, middle), BF16, BY_ROWS), ((blocks, 1, middle), F32, BY_BLOCK)]
+    dev_out_out = [((low, outputs), BF16, BY_ROWS), ((blocks, 1, outputs), F32, BY_BLOCK)]
+    hidden_out = [((low, middle), BF16, BY_ROWS)]
+    wide_out = [((low, outputs), BF16, BY_ROWS)]
+    acc_mid, acc_out = ((per_block, middle), F32), ((per_block, outputs), F32)
     unit_flops = 2 * low * middle * middle
 
-    planes, d_in1, c_in1, t_in1 = run(
-        split_kernel,
-        ins=[
-            (image_in.reshape(4 * low, inputs), "rows"),
-            (perm, "all"),
-            (mask_in, "planes"),
-            (weight_in1, "all"),
+    def normal(dev, centre, stats, gain, shift, kind=BY_ROWS):
+        return [(dev, kind), (centre, BY_BLOCK), (stats, WHOLE), (gain, WHOLE), (shift, WHOLE)]
+
+    planes, d_in1, c_in1, d_skip, c_skip, n_in1, n_skip, halo_in1, halo_c_in1 = run(
+        open_kernel,
+        [
+            (image_in.reshape(4 * low, inputs), BY_ROWS),
+            (perm, WHOLE),
+            (mask_in, BY_PLANES),
+            (mask_out, BY_ROWS),
+            (weight_in1, WHOLE),
+            (weight_skip, WHOLE),
         ],
-        outs=[
-            ((4, low, inputs), BF16, "planes"),
-            ((4, low, middle), BF16, "planes"),
-            ((blocks, 1, middle), F32, "each"),
-            ((3, middle), F32, "all"),
+        [
+            ((4, low, inputs), BF16, BY_PLANES),
+            ((4, low, middle), BF16, BY_PLANES),
+            ((blocks, 1, middle), F32, BY_BLOCK),
+        ]
+        + dev_out_out,
+        True,
+        3,
+        (middle, outputs),
+        scratch=[((4, per_block, middle), F32), acc_out],
+        flops=20 * unit_flops,
+        edges=[(1, 2, True, 1), (1, 3, True, 1)],
+        centres=(2, (1,)),
+        edge=edge,
+    )
+    hid_in1, d_mid1, c_mid1, n_mid1, halo_mid1, halo_c_mid1 = run(
+        functools.partial(mid1_kernel, rows_low),
+        [
+            (d_in1, BY_PLANES),
+            (c_in1, BY_BLOCK),
+            (mask_in, BY_PLANES),
+            (halo_in1, BY_PLANES),
+            (halo_c_in1[0], BY_BLOCK),
+            (mask_above, BY_PLANES),
+            (n_in1, WHOLE),
+            (g_in1, WHOLE),
+            (s_in1, WHOLE),
+            (mask_out, BY_ROWS),
+            (kernel_mid1, WHOLE),
         ],
-        scratch=[((4, per_block, middle), F32)],
-        flops=12 * unit_flops,
-    )
-    last = d_in1.reshape(2, 2, images, rows_low, cols_low, middle)[1, :, :, rows_low - 1]
-    halo_in1 = to_next(last.reshape(2, edge, middle), rows_n)
-    halo_c_in1 = to_next(c_in1, rows_n)
-    d_skip, c_skip, t_in1 = run(
-        skip_kernel,
-        ins=[(planes, "plane0"), (mask_out, "rows"), (weight_skip, "all"), (t_in1, "all")],
-        outs=dev_out_out[:2] + [((3, middle + outputs), F32, "all")],
-        scratch=[((per_block, outputs), F32), ((3, outputs), F32)],
-        flops=8 * unit_flops,
-    )
-    n_in1, n_skip = sync(t_in1, True, (middle, outputs))
-    hid_in1, d_mid1, c_mid1, t_mid1 = run(
-        functools.partial(mid1_kernel, rows_low),
-        ins=[
-            (d_in1, "planes"),
-            (c_in1, "each"),
-            (mask_in, "planes"),
-            (halo_in1, "planes"),
-            (halo_c_in1, "each"),
-            (mask_above, "planes"),
-            (n_in1, "all"),
-            (g_in1, "all"),
-            (s_in1, "all"),
-            (mask_out, "rows"),
-            (kernel_mid1, "all"),
+        [((4, low, middle), BF16, BY_PLANES)] + dev_mid_out,
+        True,
+        3,
+        (middle,),
+        scratch=[((5, per_block, middle), BF16), acc_mid],
+        flops=9 * unit_flops,
+        edges=[(1, None, False, -1)],
+        centres=(2, (-1,)),
+        edge=edge,
+    )
+    hid_mid1, d_out1, c_out1, n_out1 = run(
+        expand_kernel,
+        normal(d_mid1, c_mid1, n_mid1, g_mid1, s_mid1) + [(mask_out, BY_ROWS), (weight_out1, WHOLE)],
+        hidden_out + dev_out_out,
+        True,
+        3,
+        (outputs,),
+        scratch=[acc_out],
+        flops=4 * unit_flops,
+    )
+    join = normal(d_out1, c_out1, n_out1, g_out1, s_out1) + normal(d_skip, c_skip, n_skip, g_skip, s_skip)
+    both = [(1, None, True, 1), (1, None, False, -1)]
+    first_low, d_in2, c_in2, n_in2, halo_in2, halo_c_in2 = run(
+        join_kernel,
+        join + [(mask_out, BY_ROWS), (weight_in2, WHOLE)],
+        wide_out + dev_mid_out,
+        True,
+        3,
+        (middle,),
+        scratch=[acc_mid],
+        flops=4 * unit_flops,
+        edges=both,
+        centres=(2, (1, -1)),
+        edge=edge,
+    )
+
+    hid_in2, d_mid2, c_mid2, n_mid2, halo_mid2, halo_c_mid2 = run(
+        functools.partial(mid2_kernel, rows_low),
+        [
+            (d_in2, BY_ROWS),
+            (c_in2, BY_BLOCK),
+            (halo_in2, BY_PLANES),
+            (halo_c_in2, PAIR_BLOCK),
+            (mask_edges, BY_PLANES),
+            (n_in2, WHOLE),
+            (g_in2, WHOLE),
+            (s_in2, WHOLE),
+            (mask_out, BY_ROWS),
+            (kernel_mid2, WHOLE),
         ],
-        outs=[((4, low, middle), BF16, "planes")] + dev_mid_out,
-        scratch=[((5, per_block, middle), BF16), ((per_block, middle), F32)],
+        hidden_out + dev_mid_out,
+        True,
+        3,
+        (middle,),
+        scratch=[((per_block, 9 * middle), BF16), acc_mid],
         flops=9 * unit_flops,
-    )
-    n_mid1 = sync(t_mid1, True)
-    image_mid1 = d_mid1.reshape(images, rows_low, cols_low, middle)
-    halo_mid1 = to_previous(image_mid1[:, 0].reshape(edge, middle), rows_n)
-    halo_c_mid1 = to_previous(c_mid1, rows_n)
-    hid_mid1, d_out1, c_out1, t_out1 = run(
+        edges=both,
+        centres=(2, (1, -1)),
+        edge=edge,
+    )
+    hid_mid2, d_out2, c_out2, n_out2 = run(
         expand_kernel,
-        ins=[
-            (d_mid1, "rows"),
-            (c_mid1, "each"),
-            (n_mid1, "all"),
-            (g_mid1, "all"),
-            (s_mid1, "all"),
-            (mask_out, "rows"),
-            (weight_out1, "all"),
-        ],
-        outs=[((low, middle), BF16, "rows")] + dev_out_out,
-        scratch=[((per_block, outputs), F32)],
+        normal(d_mid2, c_mid2, n_mid2, g_mid2, s_mid2) + [(mask_out, BY_ROWS), (weight_out2, WHOLE)],
+        hidden_out + dev_out_out,
+        True,
+        3,
+        (outputs,),
+        scratch=[acc_out],
         flops=4 * unit_flops,
     )
-    n_out1 = sync(t_out1, True)
-    join = [
-        (d_out1, "rows"),
-        (c_out1, "each"),
-        (n_out1, "all"),
-        (g_out1, "all"),
-        (s_out1, "all"),
-        (d_skip, "rows"),
-        (c_skip, "each"),
-        (n_skip, "all"),
-        (g_skip, "all"),
-        (s_skip, "all"),
-    ]
-    first_low, d_in2, c_in2, t_in2 = run(
-        join_kernel,
-        ins=join + [(mask_out, "rows"), (weight_in2, "all")],
-        outs=[((low, outputs), BF16, "rows")] + dev_mid_out,
-        scratch=[((per_block, middle), F32)],
-        flops=4 * unit_flops,
-    )
-
-    def edges_of(x):
-        image = x.reshape(images, rows_low, cols_low, middle)
-        return jnp.stack(
-            [
-                to_next(image[:, rows_low - 1].reshape(edge, middle), rows_n),
-                to_previous(image[:, 0].reshape(edge, middle), rows_n),
-            ]
-        )
-
-    def centres_of(c):
-        return jnp.stack([to_next(c, rows_n), to_previous(c, rows_n)])
-
-    halo_in2, halo_c_in2 = edges_of(d_in2), centres_of(c_in2)
-    n_in2 = sync(t_in2, True)
-    hid_in2, d_mid2, c_mid2, t_mid2 = run(
-        functools.partial(mid2_kernel, rows_low),
-        ins=[
-            (d_in2, "rows"),
-            (c_in2, "each"),
-            (halo_in2, "planes"),
-            (halo_c_in2, "each2"),
-            (mask_edges, "planes"),
-            (n_in2, "all"),
-            (g_in2, "all"),
-            (s_in2, "all"),
-            (mask_out, "rows"),
-            (kernel_mid2, "all"),
-        ],
-        outs=[((low, middle), BF16, "rows")] + dev_mid_out,
-        scratch=[((9, per_block, middle), BF16), ((per_block, middle), F32)],
-        flops=9 * unit_flops,
-    )
-    n_mid2 = sync(t_mid2, True)
-    halo_mid2, halo_c_mid2 = edges_of(d_mid2), centres_of(c_mid2)
-    hid_mid2, d_out2, c_out2, t_out2 = run(
-        expand_kernel,
-        ins=[
-            (d_mid2, "rows"),
-            (c_mid2, "each"),
-            (n_mid2, "all"),
-            (g_mid2, "all"),
-            (s_mid2, "all"),
-            (mask_out, "rows"),
-            (weight_out2, "all"),
-        ],
-        outs=[((low, middle), BF16, "rows")] + dev_out_out,
-        scratch=[((per_block, outputs), F32)],
-        flops=4 * unit_flops,
-    )
-    n_out2 = sync(t_out2, True)
     block_out, gn_out2, z_out2 = run(
         final_kernel,
-        ins=[
-            (d_out2, "rows"),
-            (c_out2, "each"),
-            (n_out2, "all"),
-            (g_out2, "all"),
-            (s_out2, "all"),
-            (first_low, "rows"),
-            (cot, "rows"),
-            (mask_out, "rows"),
-        ],
-        outs=[
-            ((low, outputs), BF16, "rows"),
-            ((low, outputs), BF16, "rows"),
-            ((2, outputs), F32, "all"),
-        ],
-    )
-
-    z_out2 = sync(z_out2, False)
-    gn_mid_out = [((low, middle), BF16, "rows"), ((2, middle), F32, "all")]
-    ga_out2, gn_mid2, z_mid2 = run(
+        normal(d_out2, c_out2, n_out2, g_out2, s_out2)
+        + [(first_low, BY_ROWS), (cot, BY_ROWS), (mask_out, BY_ROWS)],
+        wide_out + wide_out,
+        False,
+        2,
+        (outputs,),
+    )
+
+    ga_out2, gn_mid2, z_mid2, halo_gn_mid2 = run(
         back_expand_kernel,
-        ins=[
-            (gn_out2, "rows"),
-            (d_out2, "rows"),
-            (c_out2, "each"),
-            (n_out2, "all"),
-            (g_out2, "all"),
-            (z_out2, "all"),
-            (mask_out, "rows"),
-            (weight_out2, "all"),
-            (d_mid2, "rows"),
-            (c_mid2, "each"),
-            (n_mid2, "all"),
-            (g_mid2, "all"),
-            (s_mid2, "all"),
-        ],
-        outs=[((low, outputs), BF16, "rows")] + gn_mid_out,
-        scratch=[((per_block, middle), F32)],
+        [
+            (gn_out2, BY_ROWS),
+            (d_out2, BY_ROWS),
+            (c_out2, BY_BLOCK),
+            (n_out2, WHOLE),
+            (g_out2, WHOLE),
+            (z_out2, WHOLE),
+            (mask_out, BY_ROWS),
+            (weight_out2, WHOLE),
+        ]
+        + normal(d_mid2, c_mid2, n_mid2, g_mid2, s_mid2),
+        wide_out + hidden_out,
+        False,
+        2,
+        (middle,),
+        scratch=[acc_mid],
         flops=4 * unit_flops,
-    )
-    halo_gn_mid2 = edges_of(gn_mid2)
-    z_mid2 = sync(z_mid2, False)
+        edges=both,
+        edge=edge,
+    )
     views2, gn_in2, z_in2 = run(
         functools.partial(back_mid2_kernel, rows_low),
-        ins=[
-            (gn_mid2, "rows"),
-            (d_mid2, "rows"),
-            (c_mid2, "each"),
-            (halo_gn_mid2, "planes"),
-            (halo_mid2, "planes"),
-            (halo_c_mid2, "each2"),
-            (mask_edges, "planes"),
-            (n_mid2, "all"),
-            (g_mid2, "all"),
-            (z_mid2, "all"),
-            (mask_out, "rows"),
-            (kernel_mid2, "all"),
-            (d_in2, "rows"),
-            (c_in2, "each"),
-            (n_in2, "all"),
-            (g_in2, "all"),
-            (s_in2, "all"),
-        ],
-        outs=[((low, 9 * middle), BF16, "rows")] + gn_mid_out,
-        scratch=[((per_block, middle), F32)],
+        [
+            (gn_mid2, BY_ROWS),
+            (d_mid2, BY_ROWS),
+            (c_mid2, BY_BLOCK),
+            (halo_gn_mid2, BY_PLANES),
+            (halo_mid2, BY_PLANES),
+            (halo_c_mid2, PAIR_BLOCK),
+            (mask_edges, BY_PLANES),
+            (n_mid2, WHOLE),
+            (g_mid2, WHOLE),
+            (z_mid2, WHOLE),
+            (mask_out, BY_ROWS),
+            (kernel_mid2, WHOLE),
+        ]
+        + normal(d_in2, c_in2, n_in2, g_in2, s_in2),
+        [((low, 9 * middle), BF16, BY_ROWS)] + hidden_out,
+        False,
+        2,
+        (middle,),
+        scratch=[acc_mid],
         flops=9 * unit_flops,
     )
-    z_in2 = sync(z_in2, False)
     ga_in2, gs1, z_sum1 = run(
         back_join_kernel,
-        ins=[
-            (gn_in2, "rows"),
-            (d_in2, "rows"),
-            (c_in2, "each"),
-            (n_in2, "all"),
-            (g_in2, "all"),
-            (z_in2, "all"),
-            (mask_out, "rows"),
-            (weight_in2, "all"),
-            (gn_out2, "rows"),
+        [
+            (gn_in2, BY_ROWS),
+            (d_in2, BY_ROWS),
+            (c_in2, BY_BLOCK),
+            (n_in2, WHOLE),
+            (g_in2, WHOLE),
+            (z_in2, WHOLE),
+            (mask_out, BY_ROWS),
+            (weight_in2, WHOLE),
+            (gn_out2, BY_ROWS),
         ]
         + join,
-        outs=[
-            ((low, middle), BF16, "rows"),
-            ((low, outputs), BF16, "rows"),
-            ((3, outputs), F32, "all"),
-        ],
-        scratch=[((per_block, outputs), F32)],
+        hidden_out + wide_out,
+        False,
+        3,
+        (outputs,),
+        scratch=[acc_out],
         flops=4 * unit_flops,
     )
 
-    z_sum1 = sync(z_sum1, False)
-    ga_out1, ga_skip, gn_mid1, z_mid1, grad_skip_in = run(
+    ga_out1, ga_skip, gn_mid1, grad_skip_in, z_mid1, halo_gn_mid1 = run(
         back_split_kernel,
-        ins=[
-            (gs1, "rows"),
-            (d_out1, "rows"),
-            (c_out1, "each"),
-            (n_out1, "all"),
-            (g_out1, "all"),
-            (d_skip, "rows"),
-            (c_skip, "each"),
-            (n_skip, "all"),
-            (g_skip, "all"),
-            (z_sum1, "all"),
-            (mask_out, "rows"),
-            (weight_out1, "all"),
-            (weight_skip, "all"),
-            (d_mid1, "rows"),
-            (c_mid1, "each"),
-            (n_mid1, "all"),
-            (g_mid1, "all"),
-            (s_mid1, "all"),
-        ],
-        outs=[((low, outputs), BF16, "rows"), ((low, outputs), BF16, "rows")]
-        + gn_mid_out
-        + [((low, inputs), BF16, "rows")],
-        scratch=[((per_block, middle), F32)],
+        [
+            (gs1, BY_ROWS),
+            (d_out1, BY_ROWS),
+            (c_out1, BY_BLOCK),
+            (n_out1, WHOLE),
+            (g_out1, WHOLE),
+            (d_skip, BY_ROWS),
+            (c_skip, BY_BLOCK),
+            (n_skip, WHOLE),
+            (g_skip, WHOLE),
+            (z_sum1, WHOLE),
+            (mask_out, BY_ROWS),
+            (weight_out1, WHOLE),
+            (weight_skip, WHOLE),
+        ]
+        + normal(d_mid1, c_mid1, n_mid1, g_mid1, s_mid1),
+        wide_out + wide_out + hidden_out + [((low, inputs), BF16, BY_ROWS)],
+        False,
+        2,
+        (middle,),
+        scratch=[acc_mid],
         flops=12 * unit_flops,
-    )
-    first_rows = gn_mid1.reshape(images, rows_low, cols_low, middle)[:, 0]
-    halo_gn_mid1 = to_previous(first_rows.reshape(edge, middle), rows_n)
-    z_mid1 = sync(z_mid1, False)
+        edges=[(2, None, False, -1)],
+        edge=edge,
+    )
     views1, gn_in1, z_in1 = run(
         functools.partial(back_mid1_kernel, rows_low),
-        ins=[
-            (gn_mid1, "rows"),
-            (d_mid1, "rows"),
-            (c_mid1, "each"),
-            (halo_gn_mid1, "rows"),
-            (halo_mid1, "rows"),
-            (halo_c_mid1, "each"),
-            (mask_edges[1], "rows"),
-            (n_mid1, "all"),
-            (g_mid1, "all"),
-            (z_mid1, "all"),
-            (mask_out, "rows"),
-            (kernel_mid1, "all"),
-            (d_in1, "planes"),
-            (c_in1, "each"),
-            (mask_in, "planes"),
-            (n_in1, "all"),
-            (g_in1, "all"),
-            (s_in1, "all"),
+        [
+            (gn_mid1, BY_ROWS),
+            (d_mid1, BY_ROWS),
+            (c_mid1, BY_BLOCK),
+            (halo_gn_mid1[0], BY_ROWS),
+            (halo_mid1[0], BY_ROWS),
+            (halo_c_mid1[0], BY_BLOCK),
+            (mask_edges[1], BY_ROWS),
+            (n_mid1, WHOLE),
+            (g_mid1, WHOLE),
+            (z_mid1, WHOLE),
+            (mask_out, BY_ROWS),
+            (kernel_mid1, WHOLE),
+            (d_in1, BY_PLANES),
+            (c_in1, BY_BLOCK),
+            (mask_in, BY_PLANES),
+            (n_in1, WHOLE),
+            (g_in1, WHOLE),
+            (s_in1, WHOLE),
         ],
-        outs=[
-            ((low, 4 * middle), BF16, "rows"),
-            ((4, low, middle), BF16, "planes"),
-            ((2, middle), F32, "all"),
-        ],
+        [((low, 4 * middle), BF16, BY_ROWS), ((4, low, middle), BF16, BY_PLANES)],
+        False,
+        2,
+        (middle,),
         scratch=[((4, per_block, middle), F32)],
         flops=9 * unit_flops,
     )
-    z_in1 = sync(z_in1, False)
-    ga_in1, grad_image = run(
+    ga_in1, grad_image = stage(
         back_image_kernel,
-        ins=[
-            (gn_in1, "planes"),
-            (d_in1, "planes"),
-            (c_in1, "each"),
-            (n_in1, "all"),
-            (g_in1, "all"),
-            (z_in1, "all"),
-            (mask_in, "planes"),
-            (weight_in1, "all"),
-            (grad_skip_in, "rows"),
-            (perm, "all"),
+        blocks,
+        [
+            (gn_in1, BY_PLANES),
+            (d_in1, BY_PLANES),
+            (c_in1, BY_BLOCK),
+            (n_in1, WHOLE),
+            (g_in1, WHOLE),
+            (z_in1, WHOLE),
+            (mask_in, BY_PLANES),
+            (weight_in1, WHOLE),
+            (grad_skip_in, BY_ROWS),
+            (perm, WHOLE),
         ],
-        outs=[((4, low, middle), BF16, "planes"), ((4 * low, inputs), BF16, "rows")],
+        [((4, low, middle), BF16, BY_PLANES), ((4 * low, inputs), BF16, BY_ROWS)],
         scratch=[((4, per_block, inputs), BF16)],
         flops=12 * unit_flops,
     )
-
-    def weight_term(values, upstream):
-        return lax.dot_general(
-            values, upstream, (((0,), (0,)), ((), ())), preferred_element_type=F32
-        ).astype(BF16)
-
-    def reduced(grad):
-        shard = lax.psum_scatter(grad, "img", scatter_dimension=0, tiled=True)
-        return lax.psum(shard, "rows").astype(F32)
-
-    dw_out2 = reduced(weight_term(hid_mid2, ga_out2))
-    dw_mid2 = reduced(weight_term(hid_in2, views2))
-    dw_in2 = reduced(weight_term(first_low, ga_in2))
-    dw_out1 = reduced(weight_term(hid_mid1, ga_out1))
-    dw_skip = reduced(weight_term(planes[0], ga_skip))
-    m = middle
-    dw_00 = weight_term(hid_in1[0], views1[:, m : 2 * m])
-    dw_01 = weight_term(hid_in1[1], views1[:, m : 3 * m])
-    dw_10 = weight_term(hid_in1[2], views1[:, : 2 * m])
-    dw_11 = weight_term(hid_in1[3], views1)
-    dw_mid1 = jnp.concatenate(
-        [
-            dw_11[:, 3 * m :],
-            dw_10[:, :m],
-            dw_11[:, :m],
-            dw_01[:, m:],
-            dw_00,
-            dw_01[:, :m],
-            dw_11[:, 2 * m : 3 * m],
-            dw_10[:, m:],
-            dw_11[:, m : 2 * m],
-        ],
-        axis=1,
-    )
-    dw_mid1 = reduced(dw_mid1)
-    dw_in1 = reduced(
-        weight_term(planes.reshape(4 * low, inputs), ga_in1.reshape(4 * low, middle))
-    )
+    sums = [z_in1, z_mid1, z_sum1, z_in2, z_mid2, z_out2]
+
+    if (rows_n, img_n) == (4, 8):
+        done = summed_weights(
+            rows_n,
+            run.calls,
+            [
+                hid_mid2,
+                ga_out2,
+                hid_in2,
+                views2,
+                first_low,
+                ga_in2,
+                hid_mid1,
+                ga_out1,
+                planes,
+                ga_skip,
+                hid_in1,
+                views1,
+                ga_in1,
+            ],
+        )
+        grads, rows_of = unpack(done, sums)
+        dw_in1, dw_mid1, dw_out1, dw_skip, dw_in2, dw_mid2, dw_out2 = grads
+        dw_mid1, dw_mid2 = (
+            g.reshape(3, 3, -1, middle).transpose(2, 0, 1, 3) for g in (dw_mid1, dw_mid2)
+        )
+    else:
+        def weight_term(values, upstream):
+            return lax.dot_general(
+                values, upstream, (((0,), (0,)), ((), ())), preferred_element_type=F32
+            ).astype(BF16)
+
+        def reduced(grad):
+            shard = lax.psum_scatter(grad, "img", scatter_dimension=0, tiled=True)
+            return lax.psum(shard, "rows").astype(F32)
+
+        dw_out2 = reduced(weight_term(hid_mid2, ga_out2))
+        dw_mid2 = reduced(weight_term(hid_in2, views2))
+        dw_in2 = reduced(weight_term(first_low, ga_in2))
+        dw_out1 = reduced(weight_term(hid_mid1, ga_out1))
+        dw_skip = reduced(weight_term(planes[0], ga_skip))
+        m = middle
+        dw_00 = weight_term(hid_in1[0], views1[:, m : 2 * m])
+        dw_01 = weight_term(hid_in1[1], views1[:, m : 3 * m])
+        dw_10 = weight_term(hid_in1[2], views1[:, : 2 * m])
+        dw_11 = weight_term(hid_in1[3], views1)
+        dw_mid1 = jnp.concatenate(
+            [
+                dw_11[:, 3 * m :],
+                dw_10[:, :m],
+                dw_11[:, :m],
+                dw_01[:, m:],
+                dw_00,
+                dw_01[:, :m],
+                dw_11[:, 2 * m : 3 * m],
+                dw_10[:, m:],
+                dw_11[:, m : 2 * m],
+            ],
+            axis=1,
+        )
+        dw_mid1 = reduced(dw_mid1)
+        dw_in1 = reduced(
+            weight_term(planes.reshape(4 * low, inputs), ga_in1.reshape(4 * low, middle))
+        )
+        rows_of = [x[k] for x in sums for k in range(x.shape[0])]
     kernel_shape = (middle // img_n, 3, 3, middle)
+    (
+        shift_in1_g,
+        gain_in1_g,
+        shift_mid1_g,
+        gain_mid1_g,
+        shift_sum1_g,
+        gain_out1_g,
+        gain_skip_g,
+        shift_in2_g,
+        gain_in2_g,
+        shift_mid2_g,
+        gain_mid2_g,
+        shift_out2_g,
+        gain_out2_g,
+    ) = rows_of
     return (
         block_out.reshape(images, rows_low, cols_low, outputs),
         grad_image.reshape(images, rows_here, columns, inputs),
@@ -1354,20 +1888,20 @@
         dw_in2,
         dw_mid2.reshape(kernel_shape),
         dw_out2,
-        z_in1[1],
-        z_in1[0],
-        z_mid1[1],
-        z_mid1[0],
-        z_sum1[1],
-        z_sum1[0],
-        z_sum1[2],
-        z_sum1[0],
-        z_in2[1],
-        z_in2[0],
-        z_mid2[1],
-        z_mid2[0],
-        z_out2[1],
-        z_out2[0],
+        gain_in1_g,
+        shift_in1_g,
+        gain_mid1_g,
+        shift_mid1_g,
+        gain_out1_g,
+        shift_sum1_g,
+        gain_skip_g,
+        shift_sum1_g,
+        gain_in2_g,
+        shift_in2_g,
+        gain_mid2_g,
+        shift_mid2_g,
+        gain_out2_g,
+        shift_out2_g,
     )
 
 

time: 945 us -> 534 us (0.57)
  waiting for transfers between devices: 324 us -> 0 us
  Pallas kernels: 412 us -> 503 us
  matrix products: 66.1 us -> 0 us
  local copies, waits for them, and re-layouts: 62.8 us -> 16.2 us
  starting transfers between devices: 38.3 us -> 0 us
  between operations: 15.3 us -> 1.4 us
  other arithmetic: 16.4 us -> 3.64 us
    reduce_scatter x7 -> x0, waiting for transfers between devices: 205 us -> none  [reduced(): shard = lax.psum_scatter(grad, 'img', scatter_dimension=0, tiled=True)]
    psum x1 -> x0, waiting for transfers between devices: 119 us -> none  [reduced(): return lax.psum(shard, 'rows').astype(F32)]
    pallas_call x26 -> x15, Pallas kernels: 412 us -> 503 us  [the longest x13 359 us: call(): pl.pallas_call(kernel, grid=(blocks,), in_specs=[spec_of(x.shape, kind, b...]
    dot_general x10 -> x0, matrix products: 66.1 us -> none  [weight_term(): lax.dot_general(values, upstream, (((0,), (0,)), ((), ())), preferred_ele...]
    ppermute x15 -> x0, starting transfers between devices: 37.6 us -> none  [the longest x7 27.1 us: to_next(): return lax.ppermute(x, 'rows', [(i, i + 1) for i in range(peers - 1)])]
    reshape x4 -> x0, local copies, waits for them, and re-layouts: 17.6 us -> none  [the longest x1 6.7 us: body(): kernel_mid1 = weight_mid1.reshape(middle, 9 * middle)]
    unnamed x60 -> x16, local copies, waits for them, and re-layouts: 23.8 us -> 8.75 us
  transfers between devices with their start and end apart: 23 -> 0, of which waited for: 6 -> 0; matrix products, arithmetic and copies ran while one was open for 13% -> 0% of each run, Pallas kernels for 33% -> 0%
where the time goes in v1:
time: 534 us; the launch traced here: 524 us
  Pallas kernels  503 us (94%)
  local copies, waits for them, and re-layouts  16.2 us (3%)
    pallas_call x13, Pallas kernels, call(): pl.pallas_call(kernel, grid=(blocks,), in_specs=[spec_of(x.shape, kind, b...  359 us
    pallas_call x1, Pallas kernels, summed_weights(): pl.pallas_call(functools.partial(weights_kernel, rows_n), in_specs=[pl.Bl...  141 us

profile of v1, /device:TPU:0, one launch (start us, length us, event | category | flops | bytes accessed | tf_op | source)
XLA Modules:
  0.0 524.0 jit_solution(387149363151824947)
XLA Ops:
  0.7 0.7 compare_and_fusion.3
  1.5 0.7 compare_and_fusion.7
  2.2 0.1 copy.48
  2.4 0.1 copy.50
  2.7 0.7 compare_and_fusion.1
  3.7 0.7 broadcast_compare_fusion.1
  4.8 0.2 and_convert_fusion
  5.0 0.2 reshape.842
  5.1 0.3 broadcast_and_fusion.3
  5.9 0.9 broadcast_in_dim.20.refs_6_
  6.8 1.1 broadcast_in_dim.15.refs_3_.refs_9_.refs_5_.refs_10_.refs_8_.refs_7_.refs_6_
  7.9 1.1 broadcast_in_dim.17.refs_4_.refs_6_
  8.9 1.1 broadcast_in_dim.16.refs_5_
  10.0 1.9 broadcast_in_dim.14.refs_2_.refs_14_.mask_ref
  12.0 45.1 %shard_map.416 = (bf16[4,1280,1024]{2,1,0:T(8,128)(2,1)}, bf16[4,1280,512]{2,1,0:T(8,128)(2,1)}, f32[5,1,512]{2,1,0:T(1,128)}, bf16[1280,2048]{1,0:T(8,128)(2,1)...) custom-call(bf16[5120,1024]{1,0:T(8,128)(2,1)} %bitcast.92, ...), custom_call_target="tpu_custom_call" | custom-call | flops 13421772800 | bytes 40159232 | tf_op jit(solution)/shard_map/pallas_call | solution.py:786
  57.0 34.6 %shard_map.417 = (bf16[4,1280,512]{2,1,0:T(8,128)(2,1)}, bf16[1280,512]{1,0:T(8,128)(2,1)}, f32[5,1,512]{2,1,0:T(1,128)}, f32[3,512]{1,0:T(4,128)}, bf16[1,640,5...) custom-call(bf16[4,1280,512]{2,1,0:T(8,128)(2,1)} %get-tuple-element.102.refs_0_.refs_12_.dev, ...), custom_call_target="tpu_custom_call" | custom-call | flops 6039797760 | bytes 21798912 | tf_op jit(solution)/shard_map/pallas_call | solution.py:786
  91.6 21.0 %shard_map.418 = (bf16[1280,512]{1,0:T(8,128)(2,1)}, bf16[1280,2048]{1,0:T(8,128)(2,1)}, f32[5,1,2048]{2,1,0:T(1,128)}, f32[3,2048]{1,0:T(4,128)}) custom-call(bf16[1280,512]{1,0:T(8,128)(2,1)} %get-tuple-element.107.refs_0_.refs_13_.refs_1_, f32[5,1,512]{2,1,0:T(1,128)} %get-tuple-element.108.refs_1_.refs_14_.refs_2_, ...), custom_call_target="tpu_custom_call" | custom-call | flops 2684354560 | bytes 10678272 | tf_op jit(solution)/shard_map/pallas_call | solution.py:786
  112.6 29.4 %shard_map.419 = (bf16[1280,2048]{1,0:T(8,128)(2,1)}, bf16[1280,512]{1,0:T(8,128)(2,1)}, f32[5,1,512]{2,1,0:T(1,128)}, f32[3,512]{1,0:T(4,128)}, bf16[2,640,512]{2,1,0:T(8,128)(2,1)}, /*index=5*/f32[2,5,1,512]{3,2,1,0:T(1,128)}) custom-call(bf16[1280,2048]{1,0:T(8,128)(2,1)} %get-tuple-element.110.refs_0_.refs_9_.refs_1_, ...), custom_call_target="tpu_custom_call" | custom-call | flops 2684354560 | bytes 19965952 | tf_op jit(solution)/shard_map/pallas_call | solution.py:786
  142.0 28.2 %shard_map.420 = (bf16[1280,512]{1,0:T(8,128)(2,1)}, bf16[1280,512]{1,0:T(8,128)(2,1)}, f32[5,1,512]{2,1,0:T(1,128)}, f32[3,512]{1,0:T(4,128)}, bf16[2,640,512]{2,1,0:T(8,128)(2,1)}, /*index=5*/f32[2,5,1,512]{3,2,1,0:T(1,128)}) custom-call(bf16[1280,512]{1,0:T(8,128)(2,1)} %get-tuple-element.116.refs_0_.refs_12_.refs_1_, ...), custom_call_target="tpu_custom_call" | custom-call | flops 6039797760 | bytes 11323392 | tf_op jit(solution)/shard_map/pallas_call | solution.py:786
  170.2 21.4 %shard_map.421 = (bf16[1280,512]{1,0:T(8,128)(2,1)}, bf16[1280,2048]{1,0:T(8,128)(2,1)}, f32[5,1,2048]{2,1,0:T(1,128)}, f32[3,2048]{1,0:T(4,128)}) custom-call(bf16[1280,512]{1,0:T(8,128)(2,1)} %get-tuple-element.121.refs_0_.refs_8_.refs_1_, f32[5,1,512]{2,1,0:T(1,128)} %get-tuple-element.122.refs_1_.refs_9_.refs_2_, ...), custom_call_target="tpu_custom_call" | custom-call | flops 2684354560 | bytes 10678272 | tf_op jit(solution)/shard_map/pallas_call | solution.py:786
  191.6 22.5 %shard_map.422 = (bf16[1280,2048]{1,0:T(8,128)(2,1)}, bf16[1280,2048]{1,0:T(8,128)(2,1)}, f32[2,2048]{1,0:T(2,128)}) custom-call(bf16[1280,2048]{1,0:T(8,128)(2,1)} %get-tuple-element.124.refs_0_.refs_1_, f32[5,1,2048]{2,1,0:T(1,128)} %get-tuple-element.125.refs_1_.refs_2_, f32[3,2048]{1,0:T(4,128)} %get-tuple-element.126.refs_2_.refs_3_, ...), custom_call_target="tpu_custom_call" | custom-call | bytes 26951680 | tf_op jit(solution)/shard_map/pallas_call | solution.py:786
  214.1 27.8 %shard_map.423 = (bf16[1280,2048]{1,0:T(8,128)(2,1)}, bf16[1280,512]{1,0:T(8,128)(2,1)}, f32[2,512]{1,0:T(2,128)}, bf16[2,640,512]{2,1,0:T(8,128)(2,1)}) custom-call(bf16[1280,2048]{1,0:T(8,128)(2,1)} %get-tuple-element.129.refs_0_.refs_8_, bf16[1280,2048]{1,0:T(8,128)(2,1)} %get-tuple-element.124.refs_0_.refs_1_, ...), custom_call_target="tpu_custom_call" | custom-call | flops 2684354560 | bytes 21213184 | tf_op jit(solution)/shard_map/pallas_call | solution.py:786
  241.9 22.7 %shard_map.424 = (bf16[1280,4608]{1,0:T(8,128)(2,1)}, bf16[1280,512]{1,0:T(8,128)(2,1)}, f32[2,512]{1,0:T(2,128)}) custom-call(bf16[1280,512]{1,0:T(8,128)(2,1)} %get-tuple-element.131.refs_0_, bf16[1280,512]{1,0:T(8,128)(2,1)} %get-tuple-element.121.refs_0_.refs_8_.refs_1_, f32[5,1,512]{2,1,0:T(1,128)} %get-tuple-element.122.refs_1_.refs_9_.refs_2_, ...), custom_call_target="tpu_custom_call" | custom-call | flops 6039797760 | bytes 25753600 | tf_op jit(solution)/shard_map/pallas_call | solution.py:786
  264.6 28.5 %shard_map.425 = (bf16[1280,512]{1,0:T(8,128)(2,1)}, bf16[1280,2048]{1,0:T(8,128)(2,1)}, f32[3,2048]{1,0:T(4,128)}) custom-call(bf16[1280,512]{1,0:T(8,128)(2,1)} %get-tuple-element.136.refs_0_, bf16[1280,512]{1,0:T(8,128)(2,1)} %get-tuple-element.116.refs_0_.refs_12_.refs_1_, f32[5,1,512]{2,1,0:T(1,128)} %get-tuple-element.117.refs_1_.refs_13_.refs_2_, ...), custom_call_target="tpu_custom_call" | custom-call | flops 2684354560 | bytes 27842560 | tf_op jit(solution)/shard_map/pallas_call | solution.py:786
  293.1 34.5 %shard_map.426 = (bf16[1280,2048]{1,0:T(8,128)(2,1)}, bf16[1280,2048]{1,0:T(8,128)(2,1)}, bf16[1280,512]{1,0:T(8,128)(2,1)}, bf16[1280,1024]{1,0:T(8,128)(2,1)},...) custom-call(bf16[1280,2048]{1,0:T(8,128)(2,1)} %get-tuple-element.138.refs_0_, ...), custom_call_target="tpu_custom_call" | custom-call | flops 8053063680 | bytes 38596608 | tf_op jit(solution)/shard_map/pallas_call | solution.py:786
  327.7 25.9 %shard_map.427 = (bf16[1280,2048]{1,0:T(8,128)(2,1)}, bf16[4,1280,512]{2,1,0:T(8,128)(2,1)}, f32[2,512]{1,0:T(2,128)}) custom-call(bf16[1280,512]{1,0:T(8,128)(2,1)} %get-tuple-element.140.refs_0_, bf16[1280,512]{1,0:T(8,128)(2,1)} %get-tuple-element.107.refs_0_.refs_13_.refs_1_, f32[5,1,512]{2,1,0:T(1,128)} %get-tuple-element.108.refs_1_.refs_14_.refs_2_, ...), custom_call_target="tpu_custom_call" | custom-call | flops 6039797760 | bytes 28037120 | tf_op jit(solution)/shard_map/pallas_call | solution.py:786
  353.5 17.6 %shard_map.428 = (bf16[4,1280,512]{2,1,0:T(8,128)(2,1)}, bf16[5120,1024]{1,0:T(8,128)(2,1)}) custom-call(bf16[4,1280,512]{2,1,0:T(8,128)(2,1)} %get-tuple-element.145.gn, bf16[4,1280,512]{2,1,0:T(8,128)(2,1)} %get-tuple-element.102.refs_0_.refs_12_.dev, f32[5,1,512]{2,1,0:T(1,128)} %get-tuple-element.103.refs_1_.refs_13_.centre, ...), custom_call_target="tpu_custom_call" | custom-call | flops 8053063680 | bytes 32659456 | tf_op jit(solution)/shard_map/pallas_call | solution.py:786
  371.2 141.0 %shard_map.429.done = bf16[20,64,1024]{2,1,0:T(8,128)(2,1)} custom-call(bf16[1280,512]{1,0:T(8,128)(2,1)} %get-tuple-element.149.hid_mid2, bf16[1280,2048]{1,0:T(8,128)(2,1)} %get-tuple-element.150.ga_out2, bf16[1280,512]{1,0:T(8,128)(2,1)} %get-tuple-element.151.hid_in2, bf16[1280,4608]{1,0:T(8,128)(2,1)} %get-tuple-element.152.views2, ...), custom_call_target="tpu_custom_call" | custom-call | flops 40000000000 | bytes 100000000 | tf_op jit(solution)/shard_map/pallas_call | solution.py:1376
  512.3 1.7 copy-done
  514.0 2.6 shard_map.430
  516.6 1.3 copy.53
  517.9 5.7 %copy.54 = bf16[80,2,8,2048]{3,2,1,0:T(8,128)(2,1)} copy(bf16[80,2,8,2048]{3,2,1,0:T(8,128)(2,1)} %bitcast.68) | data formatting | bytes 10485760
  (35 shorter events, 1.5 us)
Async XLA Ops:
  371.2 141.0 %copy-start.1 = (f32[2,2048]{1,0:T(2,128)S(1)}, f32[2,2048]{1,0:T(2,128)}, u32[]{:S(2)}) copy-start(f32[2,2048]{1,0:T(2,128)} %get-tuple-element.130.refs_5_) | copy-start | bytes 49156
  371.2 141.0 %copy-start.2 = (f32[3,2048]{1,0:T(4,128)S(1)}, f32[3,2048]{1,0:T(4,128)}, u32[]{:S(2)}) copy-start(f32[3,2048]{1,0:T(4,128)} %get-tuple-element.139.refs_9_.refs_2_) | copy-start | bytes 73732
  371.2 141.0 %copy-start.3 = (f32[2,512]{1,0:T(2,128)S(1)}, f32[2,512]{1,0:T(2,128)}, u32[]{:S(2)}) copy-start(f32[2,512]{1,0:T(2,128)} %get-tuple-element.137.refs_5_.refs_3_) | copy-start | bytes 12292
  371.2 141.0 %copy-start.4 = (f32[2,512]{1,0:T(2,128)S(1)}, f32[2,512]{1,0:T(2,128)}, u32[]{:S(2)}) copy-start(f32[2,512]{1,0:T(2,128)} %get-tuple-element.135.refs_9_.refs_4_) | copy-start | bytes 12292
  371.2 141.0 %copy-start.5 = (f32[2,512]{1,0:T(2,128)S(1)}, f32[2,512]{1,0:T(2,128)}, u32[]{:S(2)}) copy-start(f32[2,512]{1,0:T(2,128)} %get-tuple-element.144.refs_9_.refs_1_) | copy-start | bytes 12292
  371.2 141.0 %copy-start.6 = (f32[2,512]{1,0:T(2,128)S(1)}, f32[2,512]{1,0:T(2,128)}, u32[]{:S(2)}) copy-start(f32[2,512]{1,0:T(2,128)} %get-tuple-element.146.sums_in.refs_0_) | copy-start | bytes 12292
  512.3 1.7 copy-start
